TPU v7x, 32 devices: a whole 2x2x4 slice. The times are simulated.
32 devices in a mesh: row: 8 (over z, y), col: 4 (over x, core).
Axes of the slice: x: 2, y: 2, z: 4, core: 2. Of those that a mesh axis runs over, the one named last changes fastest.
Arguments:
- a_tiles: bfloat16 [128, 27, 128, 128], P('row'), may hold values from -0.109375 to 0.109375
- a_cols: int32 [128, 27], P('row'), may hold values from 0 to 19, as said below
- p_tiles: bfloat16 [128, 4, 128, 128], P('row', 'col'), may hold values from -2 to 2
- p_cols: int32 [128, 4], P('row', 'col'), may hold values from 0 to 15, as said below
- send_rows: int32 [16, 2], P('row'), may hold values from 0 to 15, as said below
Outputs:
- coarse_matrix: float32 [16, 16, 128, 128], P('row', 'col')
Inputs may be any that keep to these rules, and one draw needn't show every extreme that they name: `a_cols`: an entry below 16 names a fine block row of the device's own slab; an entry 16 + t with t < 2 names the t-th row that the previous slab sends to this slab, and 18 + t the t-th row that the next slab sends to it. Every slab reads all 4 rows that it receives. Slabs are periodic. `p_cols`: the coarse block column of slot k in fine block row i is congruent to k modulo 4 and lies among the 6 consecutive ids that start at ((i div 16) - 1) * 2, modulo 16. `send_rows`: each row lists 2 distinct slab-local rows.
All inputs are finite; a program needn't handle non-finite values.
Results may differ from a plain program's by a relative error of at most 0.0029.
Values may be sent and summed in bfloat16 or wider, within the bound.
A program may use at most 192 MiB of HBM per device.

v0:
```python
import jax
import jax.numpy as jnp
from jax import lax
from jax.sharding import PartitionSpec as P

CB = 2


def shifted(block, axis, distance):
    devices = range(lax.axis_size(axis))
    route = [((i - distance) % len(devices), i) for i in devices]
    return lax.ppermute(block, axis, route)


def add_terms(buffer, left_tiles, window_rows, products, column_local, column_start, span):
    height = buffer.shape[0]
    column_count = buffer.shape[1]
    row_hot = (
        window_rows[:, :, None] == jnp.arange(height, dtype=jnp.int32)[None, None, :]
    ).astype(jnp.bfloat16)
    column_place = jnp.mod(column_local - column_start, column_count)
    column_hot = (
        column_place[:, :, None] == jnp.arange(span, dtype=jnp.int32)[None, None, :]
    ).astype(jnp.bfloat16)
    grouped = jnp.einsum("img,imyz->igyz", column_hot, products, preferred_element_type=jnp.float32)
    weighted = jnp.einsum("ikr,ikyx->riyx", row_hot, left_tiles, preferred_element_type=jnp.float32)
    window = jnp.einsum("riyx,igyz->rgxz", weighted, grouped, precision=lax.Precision.HIGHEST)
    targets = jnp.mod(column_start + jnp.arange(span, dtype=jnp.int32), column_count)
    placement = (targets[:, None] == jnp.arange(column_count, dtype=jnp.int32)[None, :]).astype(
        jnp.float32
    )
    return jnp.einsum("gc,rgxz->rcxz", placement, window, precision=lax.Precision.HIGHEST)


def shards(a_tiles, a_cols, p_tiles, p_cols, send_rows):
    peer_count = lax.axis_size("row")
    quarter_count = lax.axis_size("col")
    row_index = lax.axis_index("row")
    tile_width = p_tiles.shape[-1]
    coarse_total = CB * peer_count
    column_count = coarse_total // quarter_count
    span = min(column_count, (7 * CB - 1) // quarter_count + 2)
    column_start = jnp.mod(jnp.floor_divide((row_index - 3) * CB, quarter_count), column_count)
    lower_tiles, lower_ids = shifted((p_tiles[send_rows[0]], p_cols[send_rows[0]]), "row", 1)
    upper_tiles, upper_ids = shifted((p_tiles[send_rows[1]], p_cols[send_rows[1]]), "row", -1)
    left_tiles, left_ids = (
        lax.all_gather(p_tiles, "col", axis=1, tiled=True),
        lax.all_gather(p_cols, "col", axis=1, tiled=True),
    )
    right_tiles = jnp.concatenate([p_tiles[:, 0], lower_tiles[:, 0], upper_tiles[:, 0]], axis=0)
    right_ids = jnp.concatenate([p_cols[:, 0], lower_ids[:, 0], upper_ids[:, 0]], axis=0)
    picked = right_tiles[a_cols]
    products = jnp.einsum(
        "imxy,imyz->imxz", a_tiles, picked, preferred_element_type=jnp.float32
    ).astype(jnp.bfloat16)
    column_local = right_ids[a_cols] // quarter_count
    window_rows = jnp.mod(left_ids - (row_index - 1) * CB, coarse_total)
    buffer = jnp.zeros((3 * CB, column_count, tile_width, tile_width), jnp.float32)
    buffer = add_terms(buffer, left_tiles, window_rows, products, column_local, column_start, span)
    from_lower = shifted(buffer[2 * CB :], "row", 1)
    from_upper = shifted(buffer[:CB], "row", -1)
    coarse_block = buffer[CB : 2 * CB] + from_lower + from_upper
    return coarse_block


def solution(mesh):
    in_specs = (
        P("row", None, None, None),
        P("row", None),
        P("row", "col", None, None),
        P("row", "col"),
        P("row", None),
    )
    out_specs = P("row", "col", None, None)
    return jax.shard_map(shards, mesh=mesh, in_specs=in_specs, out_specs=out_specs, check_vma=False)
```

profile of v0, /device:TPU:0, one launch (start us, length us, event | category | flops | bytes accessed | tf_op | source)
XLA Modules:
  0.0 152.7 jit_solution(11037828755479196296)
XLA Ops:
  6.5 0.0 copy-start.1
  6.5 0.0 all-gather.3.cloned.1.call-start
  6.5 0.8 fusion.26
  7.3 1.3 gather_fusion
  8.6 3.0 %collective-permute-start = (s32[2,1]{0,1:T(1,128)S(1)}, s32[2,1]{0,1:T(1,128)S(1)}, u32[]{:S(2)}, u32[]{:S(2)}) collective-permute-start(s32[2,1]{0,1:T(1,128)S(1)} %bitcast.77), channel_id=1, source_target_pairs={{28,0},{0,4},{4,8},{8,12},{12,16},{16,20},{20,24},{24,28},{29,1},{... | collective-permute-start | bytes 32 | tf_op jit(solution)/shard_map/ppermute | solution.py:12
  11.6 1.3 gather_fusion.1
  12.9 3.0 %collective-permute-start.1 = (s32[2,1]{0,1:T(1,128)S(1)}, s32[2,1]{0,1:T(1,128)S(1)}, u32[]{:S(2)}, u32[]{:S(2)}) collective-permute-start(s32[2,1]{0,1:T(1,128)S(1)} %bitcast.78), channel_id=1, source_target_pairs={{4,0},{8,4},{12,8},{16,12},{20,16},{24,20},{28,24},{0,28},{5,1},{9... | collective-permute-start | bytes 32 | tf_op jit(solution)/shard_map/ppermute | solution.py:12
  15.9 1.6 %gather_fusion.3 = bf16[2,128,128]{2,1,0:T(8,128)(2,1)S(1)} fusion(bf16[16,128,128]{2,1,0:T(8,128)(2,1)} %bitcast.66, s32[1024]{0:T(1024)S(1)} %get-tuple-element.10), kind=kCustom, calls=%fused_computation.3 | custom fusion | bytes 131080 | tf_op jit(solution)/shard_map/gather | solution.py:44
  17.5 0.1 collective-permute-start.2
  17.6 1.6 %gather_fusion.4 = bf16[2,128,128]{2,1,0:T(8,128)(2,1)S(1)} fusion(bf16[16,128,128]{2,1,0:T(8,128)(2,1)} %bitcast.67, s32[1024]{0:T(1024)S(1)} %get-tuple-element.9), kind=kCustom, calls=%fused_computation.4 | custom fusion | bytes 131080 | tf_op jit(solution)/shard_map/gather | solution.py:45
  19.2 4.8 %collective-permute-start.3 = (bf16[2,1,128,128]{3,2,0,1:T(8,128)(2,1)S(1)}, bf16[2,1,128,128]{3,2,0,1:T(8,128)(2,1)S(1)}, u32[]{:S(2)}, u32[]{:S(2)}) collective-permute-start(bf16[2,1,128,128]{3,2,0,1:T(8,128)(2,1)S(1)} %bitcast.73), channel_id=1, source_target_pairs={{4,0},{8,4},{12,8},{16,12},{20,16},{24,20},{28,24},{0,28},{5,1},{9... | collective-permute-start | bytes 196616 | tf_op jit(solution)/shard_map/ppermute | solution.py:12
  23.9 0.0 all-gather.3.cloned.1.call-update
  24.0 0.7 compare_select_fusion
  24.7 0.1 reshape.123
  24.8 5.2 %all-gather = s32[4,1,16]{2,1,0:T(1,128)S(1)} all-gather(s32[1,1,16]{2,1,0:T(1,128)} %bitcast.63), channel_id=1, replica_groups=mesh['row'=8,'col'=4] {'col'}, dimensions={0}, use_global_device_ids=true | all-gather | bytes 320 | tf_op jit(solution)/shard_map/all_gather | solution.py:48
  30.0 0.1 copy.20
  30.1 0.0 collective-permute-done
  30.1 0.0 collective-permute-done.1
  30.1 0.7 pad_add_fusion
  30.9 3.0 %gather_fusion.2 = s32[432]{0:T(512)S(1)} fusion(s32[20]{0:T(128)S(1)} %pad_add_fusion, s32[1024]{0:T(1024)S(1)} %pad_clamp_fusion), kind=kCustom, calls=%fused_computation.2 | custom fusion | bytes 5184 | tf_op jit(solution)/shard_map/gather | solution.py:56
  33.9 0.1 reshape.122
  34.0 0.0 collective-permute-done.2
  34.0 0.0 collective-permute-done.3
  34.0 0.0 copy-done.1
  34.0 0.1 pad_maximum_fusion
  34.1 13.1 %gather_fusion.5 = bf16[432,128,128]{2,1,0:T(8,128)(2,1)} fusion(bf16[20,128,128]{2,1,0:T(8,128)(2,1)S(1)} %pad_maximum_fusion, s32[1024]{0:T(1024)S(1)} %pad_clamp_fusion), kind=kCustom, calls=%fused_computation.5 | custom fusion | bytes 28313280 | tf_op jit(solution)/shard_map/gather | solution.py:52
  47.2 20.0 %convert_bitcast_fusion = bf16[16,27,128,128]{2,3,1,0:T(8,128)(2,1)} fusion(bf16[16,27,128,128]{3,2,1,0:T(8,128)(2,1)} %bitcast.65, bf16[16,27,128,128]{3,2,1,0:T(8,128)(2,1)} %param.5), kind=kOutput, calls=%fused_computation.6 | convolution fusion | flops 1819017216 | bytes 42467328 | tf_op jit(solution)/shard_map/imxy,imyz->imxz/dot_general | solution.py:53
  67.2 24.5 %copy.19 = bf16[16,27,128,128]{3,1,2,0:T(8,128)(2,1)} copy(bf16[16,27,128,128]{2,3,1,0:T(8,128)(2,1)} %convert_bitcast_fusion) | data formatting | bytes 28311552 | tf_op jit(solution)/shard_map/convert_element_type | solution.py:55
  91.8 10.0 %convolution_bitcast_fusion.1 = f32[16,4,128,128,1]{3,1,2,0,4:T(4,128)} fusion(bf16[16,27,128,128]{3,1,2,0:T(8,128)(2,1)} %copy.19, s32[16,27]{1,0:T(8,128)S(1)} %add_select_fusion), kind=kOutput, calls=%fused_computation.12 | convolution fusion | flops 56624832 | bytes 18351808 | tf_op jit(solution)/shard_map/img,imyz->igyz/dot_general | solution.py:25
  101.8 0.0 all-gather.3.cloned.1.call-done
  101.8 0.0 copy-start
  101.8 3.7 %convolution_bitcast_fusion = f32[6,16,128,128]{3,0,2,1:T(8,128)S(1)} fusion(bf16[16,4,128,128]{3,2,0,1:T(8,128)(2,1)} %all-gather.3.cloned.1.call-done, s32[16,4]{1,0:T(8,128)S(1)} %copy.20), kind=kOutput, calls=%fused_computation.11 | convolution fusion | flops 12583296 | bytes 8388864 | tf_op jit(solution)/shard_map/ikr,ikyx->riyx/dot_general | solution.py:26
  105.5 0.0 copy-done
  105.5 11.2 %fusion.5 = f32[6,4,128,128]{2,3,0,1:T(8,128)S(1)} fusion(f32[6,16,128,128]{3,0,2,1:T(8,128)S(1)} %convolution_bitcast_fusion, f32[16,4,128,128,1]{3,1,2,0,4:T(4,128)S(1)} %copy-done), kind=kOutput, calls=%fused_computation.15 | convolution fusion | flops 9663676416 | bytes 12058624 | tf_op jit(solution)/shard_map/riyx,igyz->rgxz/dot_general | solution.py:27
  116.8 0.8 copy.25
  117.5 1.7 %convolution_bitcast_fusion.2 = f32[6,4,128,128]{3,1,2,0:T(4,128)S(1)} fusion(f32[6,4,128,128]{3,1,2,0:T(4,128)S(1)} %copy.25, s32[4]{0:T(128)S(1)} %and_select_fusion), kind=kOutput, calls=%fused_computation.14 | convolution fusion | flops 18874384 | bytes 3145744 | tf_op jit(solution)/shard_map/gc,rgxz->rcxz/dot_general | solution.py:32
  119.2 0.1 fusion.28
  119.3 0.1 collective-permute-start.4
  119.4 4.7 %collective-permute-start.5 = (f32[2,4,128,128]{3,1,2,0:T(4,128)S(1)}, f32[2,4,128,128]{3,1,2,0:T(4,128)S(1)}, u32[]{:S(2)}, u32[]{:S(2)}) collective-permute-start(f32[2,4,128,128]{3,1,2,0:T(4,128)S(1)} %get-tuple-element.6), channel_id=1, source_target_pairs={{4,0},{8,4},{12,8},{16,12},{20,16},{24,20},{28,24},{0,28},{5,1},{9... | collective-permute-start | bytes 1572872 | tf_op jit(solution)/shard_map/ppermute | solution.py:12
  124.1 18.4 %collective-permute-done.4 = f32[2,4,128,128]{3,1,2,0:T(4,128)S(1)} collective-permute-done((f32[2,4,128,128]{3,1,2,0:T(4,128)S(1)}, f32[2,4,128,128]{3,1,2,0:T(4,128)S(1)}, u32[]{:S(2)}, u32[]{:S(2)}) %collective-permute-start.4) | collective-permute-done | bytes 524320 | tf_op jit(solution)/shard_map/ppermute | solution.py:12
  142.5 2.3 %collective-permute-done.5 = f32[2,4,128,128]{3,1,2,0:T(4,128)S(1)} collective-permute-done((f32[2,4,128,128]{3,1,2,0:T(4,128)S(1)}, f32[2,4,128,128]{3,1,2,0:T(4,128)S(1)}, u32[]{:S(2)}, u32[]{:S(2)}) %collective-permute-start.5) | collective-permute-done | bytes 524320 | tf_op jit(solution)/shard_map/ppermute | solution.py:12
  144.8 0.2 fusion.10
  145.0 0.8 copy.26
  (6 shorter events, 0.1 us)
Async XLA Ops:
  6.5 27.5 %copy-start.1 = (bf16[16,1,128,128]{3,2,1,0:T(8,128)(2,1)S(1)}, bf16[16,1,128,128]{3,2,1,0:T(8,128)(2,1)}, u32[]{:S(2)}) copy-start(bf16[16,1,128,128]{3,2,1,0:T(8,128)(2,1)} %param.7) | copy-start | bytes 1572868
  6.5 95.2 %all-gather.3.cloned.1.call-start = ((), (), s32[]{:S(2)}) async-start(), calls=%async_computation | async-start | bytes 2621440 | tf_op jit(solution)/shard_map/all_gather | solution.py:47
  8.6 21.5 %collective-permute-start = (s32[2,1]{0,1:T(1,128)S(1)}, s32[2,1]{0,1:T(1,128)S(1)}, u32[]{:S(2)}, u32[]{:S(2)}) collective-permute-start(s32[2,1]{0,1:T(1,128)S(1)} %bitcast.77), channel_id=1, source_target_pairs={{28,0},{0,4},{4,8},{8,12},{12,16},{16,20},{20,24},{24,28},{29,1},{... | collective-permute-start | bytes 32 | tf_op jit(solution)/shard_map/ppermute | solution.py:12
  12.9 17.3 %collective-permute-start.1 = (s32[2,1]{0,1:T(1,128)S(1)}, s32[2,1]{0,1:T(1,128)S(1)}, u32[]{:S(2)}, u32[]{:S(2)}) collective-permute-start(s32[2,1]{0,1:T(1,128)S(1)} %bitcast.78), channel_id=1, source_target_pairs={{4,0},{8,4},{12,8},{16,12},{20,16},{24,20},{28,24},{0,28},{5,1},{9... | collective-permute-start | bytes 32 | tf_op jit(solution)/shard_map/ppermute | solution.py:12
  17.5 16.5 %collective-permute-start.2 = (bf16[2,1,128,128]{3,2,0,1:T(8,128)(2,1)S(1)}, bf16[2,1,128,128]{3,2,0,1:T(8,128)(2,1)S(1)}, u32[]{:S(2)}, u32[]{:S(2)}) collective-permute-start(bf16[2,1,128,128]{3,2,0,1:T(8,128)(2,1)S(1)} %bitcast.72), channel_id=1, source_target_pairs={{28,0},{0,4},{4,8},{8,12},{12,16},{16,20},{20,24},{24,28},{29,1},{... | collective-permute-start | bytes 196616 | tf_op jit(solution)/shard_map/ppermute | solution.py:12
  19.2 14.8 %collective-permute-start.3 = (bf16[2,1,128,128]{3,2,0,1:T(8,128)(2,1)S(1)}, bf16[2,1,128,128]{3,2,0,1:T(8,128)(2,1)S(1)}, u32[]{:S(2)}, u32[]{:S(2)}) collective-permute-start(bf16[2,1,128,128]{3,2,0,1:T(8,128)(2,1)S(1)} %bitcast.73), channel_id=1, source_target_pairs={{4,0},{8,4},{12,8},{16,12},{20,16},{24,20},{28,24},{0,28},{5,1},{9... | collective-permute-start | bytes 196616 | tf_op jit(solution)/shard_map/ppermute | solution.py:12
  101.8 3.7 %copy-start = (f32[16,4,128,128,1]{3,1,2,0,4:T(4,128)S(1)}, f32[16,4,128,128,1]{3,1,2,0,4:T(4,128)}, u32[]{:S(2)}) copy-start(f32[16,4,128,128,1]{3,1,2,0,4:T(4,128)} %convolution_bitcast_fusion.1) | copy-start | bytes 12582916
  119.3 23.2 %collective-permute-start.4 = (f32[2,4,128,128]{3,1,2,0:T(4,128)S(1)}, f32[2,4,128,128]{3,1,2,0:T(4,128)S(1)}, u32[]{:S(2)}, u32[]{:S(2)}) collective-permute-start(f32[2,4,128,128]{3,1,2,0:T(4,128)S(1)} %get-tuple-element.5), channel_id=1, source_target_pairs={{28,0},{0,4},{4,8},{8,12},{12,16},{16,20},{20,24},{24,28},{29,1},{... | collective-permute-start | bytes 1572872 | tf_op jit(solution)/shard_map/ppermute | solution.py:12
  119.4 25.4 %collective-permute-start.5 = (f32[2,4,128,128]{3,1,2,0:T(4,128)S(1)}, f32[2,4,128,128]{3,1,2,0:T(4,128)S(1)}, u32[]{:S(2)}, u32[]{:S(2)}) collective-permute-start(f32[2,4,128,128]{3,1,2,0:T(4,128)S(1)} %get-tuple-element.6), channel_id=1, source_target_pairs={{4,0},{8,4},{12,8},{16,12},{20,16},{24,20},{28,24},{0,28},{5,1},{9... | collective-permute-start | bytes 1572872 | tf_op jit(solution)/shard_map/ppermute | solution.py:12
Sparse Core Ops, SparseCore 0:
  24.1 19.9 all-gather.2
where the time goes:
time: 154 us; the launch traced here: 153 us
  local copies, waits for them, and re-layouts  48.4 us (31%)
  matrix products  46.6 us (30%)
  waiting for transfers between devices  20.7 us (13%)
  starting transfers between devices  15.6 us (10%)
  between operations  13.6 us (9%)
  blocking collectives  5.18 us (3%)
  other arithmetic  2.56 us (2%)
    convert_element_type x1, local copies, waits for them, and re-layouts, shards(): products = jnp.einsum('imxy,imyz->imxz', a_tiles, picked, preferred_eleme...  24.5 us
    ppermute x6, waiting for transfers between devices, shifted(): return lax.ppermute(block, axis, route)  20.7 us
    dot_general x1, matrix products, shards(): jnp.einsum('imxy,imyz->imxz', a_tiles, picked, preferred_element_type=jnp...  20 us
    ppermute x6, starting transfers between devices, shifted(): return lax.ppermute(block, axis, route)  15.6 us
    gather x1, local copies, waits for them, and re-layouts, shards(): picked = right_tiles[a_cols]  13.1 us
    dot_general x1, matrix products, add_terms(): jnp.einsum('riyx,igyz->rgxz', weighted, grouped, precision=lax.Precision....  11.2 us
    dot_general x1, matrix products, add_terms(): jnp.einsum('img,imyz->igyz', column_hot, products, preferred_element_type...  9.99 us
    all_gather x1, blocking collectives, shards(): lax.all_gather(p_cols, 'col', axis=1, tiled=True)  5.18 us
  transfers between devices with their start and end apart: 7, of which 2 were waited for; matrix products, arithmetic and copies ran while one was open for 50% of the time, Pallas kernels for 0%

commit v1 on v0

v1 whole, which is shorter than its diff:
```python
import functools

import jax
import jax.numpy as jnp
from jax import lax
from jax.experimental import pallas as pl
from jax.experimental.pallas import tpu as pltpu
from jax.sharding import PartitionSpec as P

CB = 2
SPAN = 3
PARTS = 4
MESH = pl.DeviceIdType.MESH


def wrap(value, size):
    return jnp.where(value < 0, value + size, value)


def kernel(
    rows,
    a_cols,
    p_cols,
    send_rows,
    p_ref,
    a_ref,
    out_ref,
    a_buf,
    ghost_out,
    ghost_out_ids,
    ghost_in,
    ghost_in_ids,
    slots,
    marks,
    right,
    grouped,
    part_out,
    part_in,
    a_sem,
    ghost_send,
    ghost_recv,
    slot_send,
    slot_recv,
    mark_send,
    mark_recv,
    part_send,
    part_recv,
):
    height, entries, tile = a_buf.shape[0], a_buf.shape[1], a_buf.shape[2]
    capacity = ghost_out.shape[1]
    coarse = CB * rows
    column_count = out_ref.shape[1]
    per_part = height // PARTS
    s = lax.axis_index("row")
    k = lax.axis_index("col")
    after, before = lax.rem(s + 1, rows), lax.rem(s + rows - 1, rows)
    mate = k + 1 - 2 * lax.rem(k, 2)
    across = lax.rem(k + 2, 4)
    facing = 3 - k

    def a_copy(i):
        return pltpu.make_async_copy(a_ref.at[i], a_buf.at[i], a_sem.at[i])

    for i in range(height):
        a_copy(i).start()

    barrier = pltpu.get_barrier_semaphore()
    for device in ({"row": before}, {"row": after}, {"col": mate}, {"col": across}):
        pl.semaphore_signal(barrier, inc=1, device_id=device, device_id_type=MESH)

    def first_id(slab):
        return lax.rem(CB * slab + coarse - 4, coarse)

    def first_column(slab):
        start = first_id(slab)
        offset = lax.rem(k + 4 - lax.rem(start, 4), 4)
        return lax.rem((start + offset) // 4, column_count)

    start = first_id(s)
    left_start = lax.rem(CB * s + coarse - 2, coarse)

    for side in range(2):
        for t in range(capacity):
            row = send_rows[side, t]
            ghost_out[side, t] = p_ref[row, 0]
            ghost_out_ids[side, t : t + 1] = jnp.full((1, tile), p_cols[row, 0], jnp.int32)
    for i in range(height):
        slots[0, i // per_part, :, (i % per_part) * tile : (i % per_part + 1) * tile] = p_ref[i, 0].T
        place = wrap(p_cols[i, 0] - left_start, coarse)
        marks[0, i : i + 1] = jnp.full((1, tile), jnp.where(place >= 4, 1.0, 0.0), jnp.float32)

    pl.semaphore_wait(barrier, 4)

    def ghost_copies(side):
        target = {"row": after if side == 0 else before}
        return [
            pltpu.make_async_remote_copy(
                src_ref=src.at[side],
                dst_ref=dst.at[side],
                send_sem=ghost_send.at[side, n],
                recv_sem=ghost_recv.at[side, n],
                device_id=target,
                device_id_type=MESH,
            )
            for n, (src, dst) in enumerate(((ghost_out, ghost_in), (ghost_out_ids, ghost_in_ids)))
        ]

    hops = {1: (0, mate), 2: (0, across), 3: (2, mate)}

    def slot_copy(hop, part):
        source, target = hops[hop]
        return pltpu.make_async_remote_copy(
            src_ref=slots.at[source, part],
            dst_ref=slots.at[hop, part],
            send_sem=slot_send.at[hop - 1, part],
            recv_sem=slot_recv.at[hop - 1, part],
            device_id={"col": target},
            device_id_type=MESH,
        )

    def mark_copy(hop):
        source, target = hops[hop]
        return pltpu.make_async_remote_copy(
            src_ref=marks.at[source],
            dst_ref=marks.at[hop],
            send_sem=mark_send.at[hop - 1],
            recv_sem=mark_recv.at[hop - 1],
            device_id={"col": target},
            device_id_type=MESH,
        )

    for side in range(2):
        for copy in ghost_copies(side):
            copy.start()
    for hop in (2, 1):
        mark_copy(hop).start()
        for part in range(PARTS):
            slot_copy(hop, part).start()

    for j in range(height):
        place = wrap(p_cols[j, 0] - start, coarse)
        block = p_ref[j, 0].astype(jnp.float32)
        for g in range(SPAN):
            here = (place >= 4 * g) & (place < 4 * g + 4)
            right[j, :, g * tile : (g + 1) * tile] = (block * jnp.where(here, 1.0, 0.0)).astype(
                jnp.bfloat16
            )
    out_ref[...] = jnp.zeros_like(out_ref)
    for side in range(2):
        for copy in ghost_copies(side):
            copy.wait_recv()
        for t in range(capacity):
            place = wrap(ghost_in_ids[side, t : t + 1] - start, coarse)
            block = ghost_in[side, t].astype(jnp.float32)
            for g in range(SPAN):
                here = jnp.where((place >= 4 * g) & (place < 4 * g + 4), 1.0, 0.0)
                right[height + side * capacity + t, :, g * tile : (g + 1) * tile] = (
                    block * here
                ).astype(jnp.bfloat16)

    def forward(part):
        slot_copy(2, part).wait_recv()
        slot_copy(3, part).start()

    def multiply(i, carry):
        a_copy(i).wait()
        total = None
        for m in range(0, entries, 2):
            ms = range(m, min(m + 2, entries))
            left = jnp.concatenate([a_buf[i, n] for n in ms], axis=1)
            blocks = jnp.concatenate([right[a_cols[i, n]] for n in ms], axis=0)
            term = jnp.dot(left, blocks, preferred_element_type=jnp.float32)
            total = term if total is None else total + term
        grouped[pl.ds(pl.multiple_of(i * tile, tile), tile), :] = total.astype(jnp.bfloat16)
        return carry

    cuts = [0, 6, 11, height]
    for part in range(3):
        lax.fori_loop(cuts[part], cuts[part + 1], multiply, 0)
        if part == 0:
            mark_copy(2).wait_recv()
            mark_copy(3).start()
        forward(part)

    own_column = first_column(s)

    def part_copy(side, o):
        return pltpu.make_async_remote_copy(
            src_ref=part_out.at[side, o],
            dst_ref=part_in.at[side, o],
            send_sem=part_send.at[side, o],
            recv_sem=part_recv.at[side, o],
            device_id={"row": before if side == 0 else after},
            device_id_type=MESH,
        )

    def use_slot(index, slot):
        o = lax.rem(slot + 6 - lax.rem(CB * s, 4), 4)
        total = None
        for part in range(PARTS):
            block = slots[index, part]
            mark = jnp.concatenate(
                [marks[index, part * per_part + n : part * per_part + n + 1] for n in range(per_part)],
                axis=1,
            )
            high = (block.astype(jnp.float32) * mark).astype(jnp.bfloat16)
            left = jnp.concatenate([block - high, high], axis=0)
            depth = per_part * tile
            term = jnp.dot(
                left, grouped[part * depth : (part + 1) * depth], preferred_element_type=jnp.float32
            )
            total = term if total is None else total + term

        @pl.when(o < 2)
        def _():
            part_out[0, o] = total[:tile].astype(jnp.bfloat16)
            part_out[1, o] = total[tile:].astype(jnp.bfloat16)
            for side in range(2):
                part_copy(side, o).start()

        @pl.when(o >= 2)
        def _():
            for g in range(SPAN):
                out_ref[o - 2, lax.rem(own_column + g, column_count)] = total[
                    :tile, g * tile : (g + 1) * tile
                ]

    use_slot(0, k)
    mark_copy(1).wait_recv()
    for part in range(PARTS):
        slot_copy(1, part).wait_recv()
    use_slot(1, mate)
    forward(PARTS - 1)
    use_slot(2, across)
    mark_copy(3).wait_recv()
    for part in range(PARTS):
        slot_copy(3, part).wait_recv()
    use_slot(3, facing)

    for o in range(2):
        for side in range(2):
            part_copy(side, o).wait_recv()
            column = first_column(after if side == 0 else before)
            for g in range(SPAN):
                at = lax.rem(column + g, column_count)
                out_ref[o, at] = out_ref[o, at] + part_in[
                    side, o, :, g * tile : (g + 1) * tile
                ].astype(jnp.float32)

    for side in range(2):
        for copy in ghost_copies(side):
            copy.wait_send()
        for o in range(2):
            part_copy(side, o).wait_send()
    for hop in (1, 2, 3):
        mark_copy(hop).wait_send()
        for part in range(PARTS):
            slot_copy(hop, part).wait_send()


def shards(a_tiles, a_cols, p_tiles, p_cols, send_rows):
    rows, cols = lax.axis_size("row"), lax.axis_size("col")
    assert cols == 4
    height, entries, tile, _ = a_tiles.shape
    capacity = send_rows.shape[1]
    column_count = CB * rows // cols
    width = SPAN * tile
    smem = pl.BlockSpec(memory_space=pltpu.SMEM)
    vmem = pl.BlockSpec(memory_space=pltpu.VMEM)
    bf16, f32, i32 = jnp.bfloat16, jnp.float32, jnp.int32
    dma = pltpu.SemaphoreType.DMA
    return pl.pallas_call(
        functools.partial(kernel, rows),
        out_shape=jax.ShapeDtypeStruct((CB, column_count, tile, tile), f32),
        in_specs=[smem, smem, smem, vmem, pl.BlockSpec(memory_space=pl.ANY)],
        out_specs=vmem,
        scratch_shapes=[
            pltpu.VMEM(a_tiles.shape, bf16),
            pltpu.VMEM((2, capacity, tile, tile), bf16),
            pltpu.VMEM((2, 8, tile), i32),
            pltpu.VMEM((2, capacity, tile, tile), bf16),
            pltpu.VMEM((2, 8, tile), i32),
            pltpu.VMEM((4, PARTS, tile, height // PARTS * tile), bf16),
            pltpu.VMEM((4, height, tile), f32),
            pltpu.VMEM((height + 2 * capacity, tile, width), bf16),
            pltpu.VMEM((height * tile, width), bf16),
            pltpu.VMEM((2, CB, tile, width), bf16),
            pltpu.VMEM((2, CB, tile, width), bf16),
            dma((height,)),
            dma((2, 2)),
            dma((2, 2)),
            dma((3, PARTS)),
            dma((3, PARTS)),
            dma((3,)),
            dma((3,)),
            dma((2, CB)),
            dma((2, CB)),
        ],
        compiler_params=pltpu.CompilerParams(
            collective_id=0, has_side_effects=True, vmem_limit_bytes=48 * 1024 * 1024
        ),
        cost_estimate=pl.CostEstimate(
            flops=2 * height * entries * tile * tile * width,
            bytes_accessed=2 * a_tiles.size,
            transcendentals=0,
        ),
    )(a_cols, p_cols, send_rows, p_tiles, a_tiles)


def solution(mesh):
    in_specs = (
        P("row", None, None, None),
        P("row", None),
        P("row", "col", None, None),
        P("row", "col"),
        P("row", None),
    )
    out_specs = P("row", "col", None, None)
    return jax.shard_map(shards, mesh=mesh, in_specs=in_specs, out_specs=out_specs, check_vma=False)
```

time: 154 us -> 35.8 us (0.23)
  the two profiles are of different devices: /device:TPU:0 before, /device:TPU:2 now
where the time goes in v1:
time: 35.8 us; the launch traced here: 35.5 us
  Pallas kernels  31.6 us (88%)
  local copies, waits for them, and re-layouts  3.94 us (11%)
    pallas_call x1, Pallas kernels, shards(): pl.pallas_call(functools.partial(kernel, rows), out_shape=jax.ShapeDtypeS...  31.6 us
    unnamed x8, local copies, waits for them, and re-layouts  3.94 us

profile of v1, /device:TPU:2, one launch (start us, length us, event | category | flops | bytes accessed | tf_op | source)
XLA Modules:
  0.0 35.5 jit_solution(11834674183671926098)
XLA Ops:
  0.0 0.7 %copy.6.p_cols = s32[16,1]{1,0:T(8,128)S(1)} copy(s32[16,1]{0,1:T(1,128)} %param.8) | data formatting | bytes 128 | tf_op args[3]
  0.7 0.0 copy-start
  0.7 1.0 %copy-done = bf16[16,1,128,128]{3,2,1,0:T(8,128)(2,1)S(1)} copy-done((bf16[16,1,128,128]{3,2,1,0:T(8,128)(2,1)S(1)}, bf16[16,1,128,128]{3,2,1,0:T(8,128)(2,1)}, u32[]{:S(2)}) %copy-start) | copy-done | bytes 524312
  1.8 0.0 copy-start.1
  1.8 0.7 %copy-done.1 = s32[16,27]{1,0:T(8,128)S(1)} copy-done((s32[16,27]{1,0:T(8,128)S(1)}, s32[16,27]{1,0:T(8,128)}, u32[]{:S(2)}) %copy-start.1) | copy-done | bytes 1752
  2.5 0.0 copy-start.2
  2.5 0.7 %copy-done.2 = s32[2,2]{1,0:T(2,128)S(1)} copy-done((s32[2,2]{1,0:T(2,128)S(1)}, s32[2,2]{1,0:T(2,128)}, u32[]{:S(2)}) %copy-start.2) | copy-done | bytes 40
  3.2 31.6 %shard_map.55 = f32[2,4,128,128]{3,2,1,0:T(8,128)S(1)} custom-call(s32[16,27]{1,0:T(8,128)S(1)} %copy-done.1, s32[16,1]{1,0:T(8,128)S(1)} %copy.6.p_cols, s32[2,2]{1,0:T(2,128)S(1)} %copy-done.2, bf16[16,1,128,128]{3,2,1,0:T(8,128)(2,1)S(1)} %copy-done, bf16[16,27,128,128]{3,2,1,0:T(8,128)(2,1)} %a_ref.1), custom_call_target="tpu_custom_call" | custom-call | flops 5435817984 | bytes 14155776 | tf_op jit(solution)/shard_map/pallas_call | solution.py:272
  34.7 0.8 %copy.8 = f32[2,4,128,128]{3,2,1,0:T(8,128)} copy(f32[2,4,128,128]{3,2,1,0:T(8,128)S(1)} %shard_map.55) | data formatting | bytes 1048576
Async XLA Ops:
  0.7 1.0 %copy-start = (bf16[16,1,128,128]{3,2,1,0:T(8,128)(2,1)S(1)}, bf16[16,1,128,128]{3,2,1,0:T(8,128)(2,1)}, u32[]{:S(2)}) copy-start(bf16[16,1,128,128]{3,2,1,0:T(8,128)(2,1)} %p_ref.1) | copy-start | bytes 1572868
  1.8 0.7 %copy-start.1 = (s32[16,27]{1,0:T(8,128)S(1)}, s32[16,27]{1,0:T(8,128)}, u32[]{:S(2)}) copy-start(s32[16,27]{1,0:T(8,128)} %a_cols.1) | copy-start | bytes 5188
  2.5 0.7 %copy-start.2 = (s32[2,2]{1,0:T(2,128)S(1)}, s32[2,2]{1,0:T(2,128)}, u32[]{:S(2)}) copy-start(s32[2,2]{1,0:T(2,128)} %send_rows.1) | copy-start | bytes 52

commit v2 on v1

--- a/solution.py
+++ b/solution.py
@@ -19,12 +19,16 @@
 
 def kernel(
     rows,
+    a_cols_ref,
+    p_cols_ref,
+    send_rows_ref,
+    p_hbm,
+    a_ref,
+    out_ref,
     a_cols,
     p_cols,
     send_rows,
     p_ref,
-    a_ref,
-    out_ref,
     a_buf,
     ghost_out,
     ghost_out_ids,
@@ -36,6 +40,7 @@
     grouped,
     part_out,
     part_in,
+    small_sem,
     a_sem,
     ghost_send,
     ghost_recv,
@@ -57,10 +62,25 @@
     mate = k + 1 - 2 * lax.rem(k, 2)
     across = lax.rem(k + 2, 4)
     facing = 3 - k
+    odd = lax.rem(k, 2)
+    late = 1 - lax.rem(k // 2 + s, 2)
 
     def a_copy(i):
         return pltpu.make_async_copy(a_ref.at[i], a_buf.at[i], a_sem.at[i])
 
+    small = [
+        pltpu.make_async_copy(source, target, small_sem.at[n])
+        for n, (source, target) in enumerate(
+            (
+                (p_hbm, p_ref),
+                (send_rows_ref, send_rows),
+                (p_cols_ref, p_cols),
+                (a_cols_ref, a_cols),
+            )
+        )
+    ]
+    for copy in small:
+        copy.start()
     for i in range(height):
         a_copy(i).start()
 
@@ -79,14 +99,17 @@
     start = first_id(s)
     left_start = lax.rem(CB * s + coarse - 2, coarse)
 
+    for copy in small:
+        copy.wait()
+
     for side in range(2):
         for t in range(capacity):
             row = send_rows[side, t]
             ghost_out[side, t] = p_ref[row, 0]
-            ghost_out_ids[side, t : t + 1] = jnp.full((1, tile), p_cols[row, 0], jnp.int32)
+            ghost_out_ids[side, t : t + 1] = jnp.full((1, tile), p_cols[row], jnp.int32)
     for i in range(height):
         slots[0, i // per_part, :, (i % per_part) * tile : (i % per_part + 1) * tile] = p_ref[i, 0].T
-        place = wrap(p_cols[i, 0] - left_start, coarse)
+        place = wrap(p_cols[i] - left_start, coarse)
         marks[0, i : i + 1] = jnp.full((1, tile), jnp.where(place >= 4, 1.0, 0.0), jnp.float32)
 
     pl.semaphore_wait(barrier, 4)
@@ -132,13 +155,19 @@
     for side in range(2):
         for copy in ghost_copies(side):
             copy.start()
-    for hop in (2, 1):
+    def send_slot(hop):
         mark_copy(hop).start()
         for part in range(PARTS):
             slot_copy(hop, part).start()
 
+    @pl.when(odd == 0)
+    def _():
+        send_slot(2)
+
+    send_slot(1)
+
     for j in range(height):
-        place = wrap(p_cols[j, 0] - start, coarse)
+        place = wrap(p_cols[j] - start, coarse)
         block = p_ref[j, 0].astype(jnp.float32)
         for g in range(SPAN):
             here = (place >= 4 * g) & (place < 4 * g + 4)
@@ -174,84 +203,132 @@
         grouped[pl.ds(pl.multiple_of(i * tile, tile), tile), :] = total.astype(jnp.bfloat16)
         return carry
 
-    cuts = [0, 6, 11, height]
-    for part in range(3):
-        lax.fori_loop(cuts[part], cuts[part + 1], multiply, 0)
-        if part == 0:
-            mark_copy(2).wait_recv()
-            mark_copy(3).start()
-        forward(part)
+    lax.fori_loop(0, height // 2, multiply, 0)
+
+    @pl.when(odd == 1)
+    def _():
+        send_slot(2)
+
+    @pl.when(odd == 0)
+    def _():
+        mark_copy(2).wait_recv()
+        mark_copy(3).start()
+        forward(0)
+        forward(1)
+
+    lax.fori_loop(height // 2, height * 3 // 4, multiply, 0)
+
+    @pl.when(odd == 0)
+    def _():
+        forward(2)
+        forward(3)
+
+    lax.fori_loop(height * 3 // 4, height, multiply, 0)
 
     own_column = first_column(s)
 
-    def part_copy(side, o):
+    def part_copy(side, o, count):
         return pltpu.make_async_remote_copy(
-            src_ref=part_out.at[side, o],
-            dst_ref=part_in.at[side, o],
+            src_ref=part_out.at[side, o, pl.ds(0, count)],
+            dst_ref=part_in.at[side, o, pl.ds(0, count)],
             send_sem=part_send.at[side, o],
             recv_sem=part_recv.at[side, o],
             device_id={"row": before if side == 0 else after},
             device_id_type=MESH,
         )
 
-    def use_slot(index, slot):
-        o = lax.rem(slot + 6 - lax.rem(CB * s, 4), 4)
+    def facing_ready():
+        mark_copy(3).wait_recv()
+        for part in range(PARTS):
+            slot_copy(3, part).wait_recv()
+
+    def even_ready():
+        @pl.when(odd == 1)
+        def _():
+            facing_ready()
+
+    def odd_ready():
+        @pl.when(odd == 1)
+        def _():
+            mark_copy(2).wait_recv()
+            mark_copy(3).start()
+            for part in range(PARTS):
+                forward(part)
+
+        @pl.when(odd == 0)
+        def _():
+            facing_ready()
+
+    def use_slot(index, o):
         total = None
         for part in range(PARTS):
-            block = slots[index, part]
-            mark = jnp.concatenate(
-                [marks[index, part * per_part + n : part * per_part + n + 1] for n in range(per_part)],
-                axis=1,
-            )
-            high = (block.astype(jnp.float32) * mark).astype(jnp.bfloat16)
-            left = jnp.concatenate([block - high, high], axis=0)
+            left = slots[index, part]
+            if o < 2:
+                mark = jnp.concatenate(
+                    [marks[index, part * per_part + n : part * per_part + n + 1] for n in range(per_part)],
+                    axis=1,
+                )
+                high = (left.astype(jnp.float32) * mark).astype(jnp.bfloat16)
+                left = jnp.concatenate([left - high, high], axis=0)
             depth = per_part * tile
             term = jnp.dot(
                 left, grouped[part * depth : (part + 1) * depth], preferred_element_type=jnp.float32
             )
             total = term if total is None else total + term
-
-        @pl.when(o < 2)
+        for g in range(SPAN):
+            columns = slice(g * tile, (g + 1) * tile)
+            if o < 2:
+                part_out[0, o, g] = total[:tile, columns].astype(jnp.bfloat16)
+                part_out[1, o, g] = total[tile:, columns].astype(jnp.bfloat16)
+            else:
+                out_ref[o - 2, lax.rem(own_column + g, column_count)] = total[:, columns]
+        if o < 2:
+            for count in (SPAN, SPAN - 1):
+
+                @pl.when(late == (1 if count == SPAN else 0))
+                def _():
+                    for side in range(2):
+                        part_copy(side, o, count).start()
+
+    def when_late(value, action):
+        @pl.when(late == value)
         def _():
-            part_out[0, o] = total[:tile].astype(jnp.bfloat16)
-            part_out[1, o] = total[tile:].astype(jnp.bfloat16)
-            for side in range(2):
-                part_copy(side, o).start()
-
-        @pl.when(o >= 2)
-        def _():
-            for g in range(SPAN):
-                out_ref[o - 2, lax.rem(own_column + g, column_count)] = total[
-                    :tile, g * tile : (g + 1) * tile
-                ]
-
-    use_slot(0, k)
+            action()
+
     mark_copy(1).wait_recv()
     for part in range(PARTS):
         slot_copy(1, part).wait_recv()
-    use_slot(1, mate)
-    forward(PARTS - 1)
-    use_slot(2, across)
-    mark_copy(3).wait_recv()
-    for part in range(PARTS):
-        slot_copy(3, part).wait_recv()
-    use_slot(3, facing)
-
-    for o in range(2):
+    when_late(1, even_ready)
+    use_slot(2 * late + odd, 0)
+    when_late(1, odd_ready)
+    use_slot(2 * late + 1 - odd, 1)
+    when_late(0, even_ready)
+    use_slot(2 - 2 * late + odd, 2)
+    when_late(0, odd_ready)
+    use_slot(3 - 2 * late - odd, 3)
+
+    def collect(count):
+        for o in range(2):
+            for side in range(2):
+                part_copy(side, o, count).wait_recv()
+                column = first_column(after if side == 0 else before)
+                for g in range(count):
+                    at = lax.rem(column + g, column_count)
+                    out_ref[o, at] = out_ref[o, at] + part_in[side, o, g].astype(jnp.float32)
+
+    when_late(0, lambda: collect(SPAN))
+    when_late(1, lambda: collect(SPAN - 1))
+
+    def sent(count):
         for side in range(2):
-            part_copy(side, o).wait_recv()
-            column = first_column(after if side == 0 else before)
-            for g in range(SPAN):
-                at = lax.rem(column + g, column_count)
-                out_ref[o, at] = out_ref[o, at] + part_in[
-                    side, o, :, g * tile : (g + 1) * tile
-                ].astype(jnp.float32)
-
+            for o in range(2):
+                part_copy(side, o, count).wait_send()
+
+    when_late(1, lambda: sent(SPAN))
+    when_late(0, lambda: sent(SPAN - 1))
     for side in range(2):
         for copy in ghost_copies(side):
             copy.wait_send()
-        for o in range(2):
-            part_copy(side, o).wait_send()
     for hop in (1, 2, 3):
         mark_copy(hop).wait_send()
         for part in range(PARTS):
@@ -265,16 +342,19 @@
     capacity = send_rows.shape[1]
     column_count = CB * rows // cols
     width = SPAN * tile
-    smem = pl.BlockSpec(memory_space=pltpu.SMEM)
     vmem = pl.BlockSpec(memory_space=pltpu.VMEM)
     bf16, f32, i32 = jnp.bfloat16, jnp.float32, jnp.int32
     dma = pltpu.SemaphoreType.DMA
     return pl.pallas_call(
         functools.partial(kernel, rows),
         out_shape=jax.ShapeDtypeStruct((CB, column_count, tile, tile), f32),
-        in_specs=[smem, smem, smem, vmem, pl.BlockSpec(memory_space=pl.ANY)],
+        in_specs=[pl.BlockSpec(memory_space=pltpu.HBM)] * 5,
         out_specs=vmem,
         scratch_shapes=[
+            pltpu.SMEM(a_cols.shape, i32),
+            pltpu.SMEM((height,), i32),
+            pltpu.SMEM(send_rows.shape, i32),
+            pltpu.VMEM(p_tiles.shape, bf16),
             pltpu.VMEM(a_tiles.shape, bf16),
             pltpu.VMEM((2, capacity, tile, tile), bf16),
             pltpu.VMEM((2, 8, tile), i32),
@@ -284,8 +364,9 @@
             pltpu.VMEM((4, height, tile), f32),
             pltpu.VMEM((height + 2 * capacity, tile, width), bf16),
             pltpu.VMEM((height * tile, width), bf16),
-            pltpu.VMEM((2, CB, tile, width), bf16),
-            pltpu.VMEM((2, CB, tile, width), bf16),
+            pltpu.VMEM((2, CB, SPAN, tile, tile), bf16),
+            pltpu.VMEM((2, CB, SPAN, tile, tile), bf16),
+            dma((4,)),
             dma((height,)),
             dma((2, 2)),
             dma((2, 2)),
@@ -297,14 +378,14 @@
             dma((2, CB)),
         ],
         compiler_params=pltpu.CompilerParams(
-            collective_id=0, has_side_effects=True, vmem_limit_bytes=48 * 1024 * 1024
+            collective_id=0, has_side_effects=True, vmem_limit_bytes=64 * 1024 * 1024
         ),
         cost_estimate=pl.CostEstimate(
             flops=2 * height * entries * tile * tile * width,
             bytes_accessed=2 * a_tiles.size,
             transcendentals=0,
         ),
-    )(a_cols, p_cols, send_rows, p_tiles, a_tiles)
+    )(a_cols, p_cols.reshape(height), send_rows, p_tiles, a_tiles)
 
 
 def solution(mesh):

time: 35.8 us -> 34.8 us (0.972)
  the two profiles are of different devices: /device:TPU:2 before, /device:TPU:0 now
where the time goes in v2:
time: 34.8 us; the launch traced here: 34.6 us
  Pallas kernels  32.7 us (94%)
  local copies, waits for them, and re-layouts  1.87 us (5%)
    pallas_call x1, Pallas kernels, shards(): pl.pallas_call(functools.partial(kernel, rows), out_shape=jax.ShapeDtypeS...  32.7 us
    unnamed x1, local copies, waits for them, and re-layouts  1.87 us

profile of v2, /device:TPU:0, one launch (start us, length us, event | category | flops | bytes accessed | tf_op | source)
XLA Modules:
  0.0 34.6 jit_solution(1006580429628315819)
XLA Ops:
  0.0 32.7 %shard_map.55 = f32[2,4,128,128]{3,2,1,0:T(8,128)} custom-call(s32[16,27]{1,0:T(8,128)} %a_cols_ref.1, s32[16]{0:T(128)} %bitcast.1, s32[2,2]{1,0:T(2,128)} %send_rows_ref.1, bf16[16,1,128,128]{3,2,1,0:T(8,128)(2,1)} %p_hbm.1, bf16[16,27,128,128]{3,2,1,0:T(8,128)(2,1)} %a_ref.1), custom_call_target="tpu_custom_call" | custom-call | flops 5435817984 | bytes 14155776 | tf_op jit(solution)/shard_map/pallas_call | solution.py:348
  32.8 1.9 %copy.7 = f32[2,4,128,128]{3,2,1,0:T(8,128)} copy(f32[2,4,128,128]{3,2,1,0:T(8,128)} %shard_map.55) | data formatting | bytes 1048576

commit v3 on v2

--- a/solution.py
+++ b/solution.py
@@ -36,11 +36,15 @@
     ghost_in_ids,
     slots,
     marks,
-    right,
+    blocks,
+    running,
+    table_v,
+    table,
     grouped,
     part_out,
     part_in,
     small_sem,
+    table_sem,
     a_sem,
     ghost_send,
     ghost_recv,
@@ -166,41 +170,80 @@
 
     send_slot(1)
 
+    zero_block = height + 2 * capacity
+    pairs = (entries + SPAN) // 2
+    listed = a_cols[...]
+    group = jnp.zeros_like(listed)
+
+    def place_group(place):
+        return jnp.where(place >= 4, 1, 0) + jnp.where(place >= 8, 1, 0)
+
     for j in range(height):
-        place = wrap(p_cols[j] - start, coarse)
-        block = p_ref[j, 0].astype(jnp.float32)
-        for g in range(SPAN):
-            here = (place >= 4 * g) & (place < 4 * g + 4)
-            right[j, :, g * tile : (g + 1) * tile] = (block * jnp.where(here, 1.0, 0.0)).astype(
-                jnp.bfloat16
-            )
+        blocks[j] = p_ref[j, 0]
+        group = group + jnp.where(listed == j, place_group(wrap(p_cols[j] - start, coarse)), 0)
+    blocks[zero_block] = jnp.zeros_like(blocks[zero_block])
+    running[pairs] = jnp.zeros_like(running[pairs])
     out_ref[...] = jnp.zeros_like(out_ref)
     for side in range(2):
         for copy in ghost_copies(side):
             copy.wait_recv()
         for t in range(capacity):
-            place = wrap(ghost_in_ids[side, t : t + 1] - start, coarse)
-            block = ghost_in[side, t].astype(jnp.float32)
-            for g in range(SPAN):
-                here = jnp.where((place >= 4 * g) & (place < 4 * g + 4), 1.0, 0.0)
-                right[height + side * capacity + t, :, g * tile : (g + 1) * tile] = (
-                    block * here
-                ).astype(jnp.bfloat16)
+            j = height + side * capacity + t
+            blocks[j] = ghost_in[side, t]
+            place = wrap(ghost_in_ids[side, t : t + 1, :entries] - start, coarse)
+            group = group + jnp.where(listed == j, place_group(place), 0)
+
+    lane = lax.broadcasted_iota(jnp.int32, listed.shape, 1)
+    rank = jnp.zeros_like(listed)
+    counts = [jnp.zeros((height, 1), jnp.int32) for _ in range(SPAN)]
+    for m in range(entries):
+        one = group[:, m : m + 1]
+        rank = rank + jnp.where((group == one) & (lane > m), 1, 0)
+        counts = [counts[g] + jnp.where(one == g, 1, 0) for g in range(SPAN)]
+    sizes = [((c + 1) >> 1) << 1 for c in counts]
+    starts = [jnp.zeros_like(sizes[0]), sizes[0], sizes[0] + sizes[1]]
+    slot = rank
+    for g in range(SPAN):
+        slot = slot + jnp.where(group == g, starts[g], 0)
+    wide = table_v.shape[1:]
+    place = lax.broadcasted_iota(jnp.int32, wide, 1)
+    chosen = jnp.zeros(wide, jnp.int32)
+    column = jnp.full(wide, zero_block, jnp.int32)
+    for m in range(entries):
+        here = slot[:, m : m + 1] == place
+        chosen = chosen + jnp.where(here, m, 0)
+        column = column + jnp.where(here, listed[:, m : m + 1] - zero_block, 0)
+    going = jnp.ones(wide, jnp.int32)
+    for g in range(SPAN):
+        going = jnp.where(2 * place == starts[g], 0, going)
+        last = jnp.where(counts[g] > 0, ((starts[g] + sizes[g]) >> 1) - 1, pairs)
+        going = jnp.where(place == 64 + g, last, going)
+    table_v[0] = chosen
+    table_v[1] = column
+    table_v[2] = going
+    table_copy = pltpu.make_async_copy(table_v, table, table_sem)
+    table_copy.start()
+    table_copy.wait()
 
     def forward(part):
         slot_copy(2, part).wait_recv()
         slot_copy(3, part).start()
 
+    for i in range(height):
+        a_copy(i).wait()
+
     def multiply(i, carry):
-        a_copy(i).wait()
         total = None
-        for m in range(0, entries, 2):
-            ms = range(m, min(m + 2, entries))
-            left = jnp.concatenate([a_buf[i, n] for n in ms], axis=1)
-            blocks = jnp.concatenate([right[a_cols[i, n]] for n in ms], axis=0)
-            term = jnp.dot(left, blocks, preferred_element_type=jnp.float32)
-            total = term if total is None else total + term
-        grouped[pl.ds(pl.multiple_of(i * tile, tile), tile), :] = total.astype(jnp.bfloat16)
+        for pair in range(pairs):
+            at = (2 * pair, 2 * pair + 1)
+            left = jnp.concatenate([a_buf[i, table[0, i, n]] for n in at], axis=1)
+            right = jnp.concatenate([blocks[table[1, i, n]] for n in at], axis=0)
+            term = jnp.dot(left, right, preferred_element_type=jnp.float32)
+            total = term if pair == 0 else jnp.where(table[2, i, pair] > 0, total, 0.0) + term
+            running[pair] = total
+        rows_of = pl.ds(pl.multiple_of(i * tile, tile), tile)
+        for g in range(SPAN):
+            grouped[rows_of, g * tile : (g + 1) * tile] = running[table[2, i, 64 + g]].astype(jnp.bfloat16)
         return carry
 
     lax.fori_loop(0, height // 2, multiply, 0)
@@ -343,6 +386,7 @@
     column_count = CB * rows // cols
     width = SPAN * tile
     vmem = pl.BlockSpec(memory_space=pltpu.VMEM)
+    operands = (a_cols, p_cols.reshape(height), send_rows, p_tiles, a_tiles)
     bf16, f32, i32 = jnp.bfloat16, jnp.float32, jnp.int32
     dma = pltpu.SemaphoreType.DMA
     return pl.pallas_call(
@@ -351,7 +395,7 @@
         in_specs=[pl.BlockSpec(memory_space=pltpu.HBM)] * 5,
         out_specs=vmem,
         scratch_shapes=[
-            pltpu.SMEM(a_cols.shape, i32),
+            pltpu.VMEM(a_cols.shape, i32),
             pltpu.SMEM((height,), i32),
             pltpu.SMEM(send_rows.shape, i32),
             pltpu.VMEM(p_tiles.shape, bf16),
@@ -362,11 +406,15 @@
             pltpu.VMEM((2, 8, tile), i32),
             pltpu.VMEM((4, PARTS, tile, height // PARTS * tile), bf16),
             pltpu.VMEM((4, height, tile), f32),
-            pltpu.VMEM((height + 2 * capacity, tile, width), bf16),
+            pltpu.VMEM((height + 2 * capacity + 1, tile, tile), bf16),
+            pltpu.VMEM(((entries + SPAN) // 2 + 1, tile, tile), f32),
+            pltpu.VMEM((3, height, 128), i32),
+            pltpu.SMEM((3, height, 128), i32),
             pltpu.VMEM((height * tile, width), bf16),
             pltpu.VMEM((2, CB, SPAN, tile, tile), bf16),
             pltpu.VMEM((2, CB, SPAN, tile, tile), bf16),
             dma((4,)),
+            dma,
             dma((height,)),
             dma((2, 2)),
             dma((2, 2)),
@@ -378,14 +426,14 @@
             dma((2, CB)),
         ],
         compiler_params=pltpu.CompilerParams(
-            collective_id=0, has_side_effects=True, vmem_limit_bytes=64 * 1024 * 1024
+            collective_id=0, has_side_effects=True, vmem_limit_bytes=48 * 1024 * 1024
         ),
         cost_estimate=pl.CostEstimate(
             flops=2 * height * entries * tile * tile * width,
             bytes_accessed=2 * a_tiles.size,
             transcendentals=0,
         ),
-    )(a_cols, p_cols.reshape(height), send_rows, p_tiles, a_tiles)
+    )(*(pltpu.with_memory_space_constraint(x, pltpu.HBM) for x in operands))
 
 
 def solution(mesh):

time: 34.8 us -> 32.4 us (0.931)
  Pallas kernels: 32.7 us -> 31.4 us
  local copies, waits for them, and re-layouts: 1.87 us -> 0.8 us
    pallas_call x1, Pallas kernels: 32.7 us -> 31.4 us  [shards(): pl.pallas_call(functools.partial(kernel, rows), out_shape=jax.ShapeDtypeS...]
    unnamed x1, local copies, waits for them, and re-layouts: 1.87 us -> 0.8 us
where the time goes in v3:
time: 32.4 us; the launch traced here: 32.2 us
  Pallas kernels  31.4 us (97%)
  local copies, waits for them, and re-layouts  0.8 us (2%)
    pallas_call x1, Pallas kernels, shards(): pl.pallas_call(functools.partial(kernel, rows), out_shape=jax.ShapeDtypeS...  31.4 us
    unnamed x1, local copies, waits for them, and re-layouts  0.8 us

profile of v3, /device:TPU:0, one launch (start us, length us, event | category | flops | bytes accessed | tf_op | source)
XLA Modules:
  0.0 32.2 jit_solution(6026749751375122512)
XLA Ops:
  0.0 31.4 %shard_map.55 = f32[2,4,128,128]{3,2,1,0:T(8,128)S(1)} custom-call(s32[16,27]{1,0:T(8,128)} %a_cols_ref.1, s32[16]{0:T(128)} %bitcast.1, s32[2,2]{1,0:T(2,128)} %send_rows_ref.1, bf16[16,1,128,128]{3,2,1,0:T(8,128)(2,1)} %p_hbm.1, bf16[16,27,128,128]{3,2,1,0:T(8,128)(2,1)} %a_ref.1), custom_call_target="tpu_custom_call" | custom-call | flops 5435817984 | bytes 14155776 | tf_op jit(solution)/shard_map/pallas_call | solution.py:392
  31.4 0.8 %copy.7 = f32[2,4,128,128]{3,2,1,0:T(8,128)} copy(f32[2,4,128,128]{3,2,1,0:T(8,128)S(1)} %shard_map.55) | data formatting | bytes 1048576

commit v4 on v3

--- a/solution.py
+++ b/solution.py
@@ -69,6 +69,10 @@
     odd = lax.rem(k, 2)
     late = 1 - lax.rem(k // 2 + s, 2)
 
+    barrier = pltpu.get_barrier_semaphore()
+    for device in ({"row": before}, {"row": after}, {"col": mate}, {"col": across}):
+        pl.semaphore_signal(barrier, inc=1, device_id=device, device_id_type=MESH)
+
     def a_copy(i):
         return pltpu.make_async_copy(a_ref.at[i], a_buf.at[i], a_sem.at[i])
 
@@ -87,10 +91,6 @@
         copy.start()
     for i in range(height):
         a_copy(i).start()
-
-    barrier = pltpu.get_barrier_semaphore()
-    for device in ({"row": before}, {"row": after}, {"col": mate}, {"col": across}):
-        pl.semaphore_signal(barrier, inc=1, device_id=device, device_id_type=MESH)
 
     def first_id(slab):
         return lax.rem(CB * slab + coarse - 4, coarse)
@@ -223,6 +223,11 @@
     table_v[2] = going
     table_copy = pltpu.make_async_copy(table_v, table, table_sem)
     table_copy.start()
+
+    @pl.when(odd == 1)
+    def _():
+        send_slot(2)
+
     table_copy.wait()
 
     def forward(part):
@@ -248,10 +253,6 @@
 
     lax.fori_loop(0, height // 2, multiply, 0)
 
-    @pl.when(odd == 1)
-    def _():
-        send_slot(2)
-
     @pl.when(odd == 0)
     def _():
         mark_copy(2).wait_recv()
@@ -267,6 +268,13 @@
         forward(3)
 
     lax.fori_loop(height * 3 // 4, height, multiply, 0)
+
+    @pl.when(odd == 1)
+    def _():
+        mark_copy(2).wait_recv()
+        mark_copy(3).start()
+        for part in range(PARTS - 1):
+            forward(part)
 
     own_column = first_column(s)
 
@@ -293,10 +301,7 @@
     def odd_ready():
         @pl.when(odd == 1)
         def _():
-            mark_copy(2).wait_recv()
-            mark_copy(3).start()
-            for part in range(PARTS):
-                forward(part)
+            forward(PARTS - 1)
 
         @pl.when(odd == 0)
         def _():

time: 32.4 us -> 32.3 us (level)
  no operation moved by 1% of the time
where the time goes in v4:
time: 32.3 us; the launch traced here: 32.1 us
  Pallas kernels  31.3 us (97%)
  local copies, waits for them, and re-layouts  0.8 us (2%)
    pallas_call x1, Pallas kernels, shards(): pl.pallas_call(functools.partial(kernel, rows), out_shape=jax.ShapeDtypeS...  31.3 us
    unnamed x1, local copies, waits for them, and re-layouts  0.8 us

profile of v4, /device:TPU:0, one launch (start us, length us, event | category | flops | bytes accessed | tf_op | source)
XLA Modules:
  0.0 32.1 jit_solution(6847637426334512754)
XLA Ops:
  0.0 31.3 %shard_map.55 = f32[2,4,128,128]{3,2,1,0:T(8,128)S(1)} custom-call(s32[16,27]{1,0:T(8,128)} %a_cols_ref.1, s32[16]{0:T(128)} %bitcast.1, s32[2,2]{1,0:T(2,128)} %send_rows_ref.1, bf16[16,1,128,128]{3,2,1,0:T(8,128)(2,1)} %p_hbm.1, bf16[16,27,128,128]{3,2,1,0:T(8,128)(2,1)} %a_ref.1), custom_call_target="tpu_custom_call" | custom-call | flops 5435817984 | bytes 14155776 | tf_op jit(solution)/shard_map/pallas_call | solution.py:397
  31.3 0.8 %copy.7 = f32[2,4,128,128]{3,2,1,0:T(8,128)} copy(f32[2,4,128,128]{3,2,1,0:T(8,128)S(1)} %shard_map.55) | data formatting | bytes 1048576

commit v5 on v3

v5 whole, which is shorter than its diff:
```python
import functools

import jax
import jax.numpy as jnp
from jax import lax
from jax.experimental import pallas as pl
from jax.experimental.pallas import tpu as pltpu
from jax.sharding import PartitionSpec as P

CB = 2
SPAN = 3
PARTS = 4
MESH = pl.DeviceIdType.MESH


def wrap(value, size):
    return jnp.where(value < 0, value + size, value)


def kernel(
    rows,
    a_cols_ref,
    p_cols_ref,
    send_rows_ref,
    p_hbm,
    a_ref,
    out_ref,
    a_cols,
    p_cols,
    send_rows,
    p_ref,
    a_buf,
    ghost_out,
    ghost_out_ids,
    ghost_in,
    ghost_in_ids,
    slots,
    marks,
    blocks,
    running,
    padded,
    table_v,
    table,
    grouped,
    part_out,
    part_in,
    small_sem,
    table_sem,
    a_sem,
    ghost_send,
    ghost_recv,
    slot_send,
    slot_recv,
    mark_send,
    mark_recv,
    part_send,
    part_recv,
):
    height, entries, tile = a_buf.shape[0], a_buf.shape[1], a_buf.shape[2]
    capacity = ghost_out.shape[1]
    coarse = CB * rows
    column_count = out_ref.shape[1]
    per_part = height // PARTS
    zero_block = height + 2 * capacity
    pairs = (entries + SPAN) // 2
    s = lax.axis_index("row")
    k = lax.axis_index("col")
    after, before = lax.rem(s + 1, rows), lax.rem(s + rows - 1, rows)
    mate = k + 1 - 2 * lax.rem(k, 2)
    across = lax.rem(k + 2, 4)
    odd = lax.rem(k, 2)
    late = 1 - lax.rem(k // 2 + s, 2)

    barrier = pltpu.get_barrier_semaphore()
    for device in ({"row": before}, {"row": after}, {"col": mate}, {"col": across}):
        pl.semaphore_signal(barrier, inc=1, device_id=device, device_id_type=MESH)

    small = [
        pltpu.make_async_copy(source, target, small_sem.at[n])
        for n, (source, target) in enumerate(
            (
                (p_hbm, p_ref),
                (send_rows_ref, send_rows),
                (p_cols_ref, p_cols),
                (a_cols_ref, a_cols),
            )
        )
    ]
    for copy in small:
        copy.start()

    def a_copy(i):
        return pltpu.make_async_copy(a_ref.at[i], a_buf.at[i], a_sem.at[i])

    def start_a(i, carry):
        a_copy(i).start()
        return carry

    def wait_a(i, carry):
        a_copy(i).wait()
        return carry

    lax.fori_loop(0, height // 2, start_a, 0)

    def first_id(slab):
        return lax.rem(CB * slab + coarse - 4, coarse)

    def first_column(slab):
        start = first_id(slab)
        offset = lax.rem(k + 4 - lax.rem(start, 4), 4)
        return lax.rem((start + offset) // 4, column_count)

    def place_group(place):
        return jnp.where(place >= 4, 1, 0) + jnp.where(place >= 8, 1, 0)

    start = first_id(s)
    left_start = lax.rem(CB * s + coarse - 2, coarse)
    for copy in small:
        copy.wait()

    for side in range(2):
        for t in range(capacity):
            row = send_rows[side, t]
            ghost_out[side, t] = p_ref[row, 0]
            ghost_out_ids[side, t : t + 1] = jnp.full((1, tile), p_cols[row], jnp.int32)
    padded[...] = jnp.zeros_like(padded)
    padded[:, :entries] = a_cols[...]
    listed = padded[...]

    def own_part(part, group):
        for n in range(per_part):
            i = part * per_part + n
            block = p_ref[i, 0]
            blocks[i] = block
            slots[0, part, :, n * tile : (n + 1) * tile] = block.T
            place = wrap(p_cols[i] - left_start, coarse)
            marks[0, pl.ds(i, 1)] = jnp.full((1, tile), jnp.where(place >= 4, 1.0, 0.0), jnp.float32)
            group = group + jnp.where(listed == i, place_group(wrap(p_cols[i] - start, coarse)), 0)
        return group

    group = lax.fori_loop(0, PARTS, own_part, jnp.zeros_like(listed))

    pl.semaphore_wait(barrier, 4)

    def ghost_copies(side):
        target = {"row": after if side == 0 else before}
        return [
            pltpu.make_async_remote_copy(
                src_ref=src.at[side],
                dst_ref=dst.at[side],
                send_sem=ghost_send.at[side, n],
                recv_sem=ghost_recv.at[side, n],
                device_id=target,
                device_id_type=MESH,
            )
            for n, (src, dst) in enumerate(((ghost_out, ghost_in), (ghost_out_ids, ghost_in_ids)))
        ]

    hops = {1: (0, mate), 2: (0, across), 3: (2, mate)}

    def slot_copy(hop, part):
        source, target = hops[hop]
        return pltpu.make_async_remote_copy(
            src_ref=slots.at[source, part],
            dst_ref=slots.at[hop, part],
            send_sem=slot_send.at[hop - 1, part],
            recv_sem=slot_recv.at[hop - 1, part],
            device_id={"col": target},
            device_id_type=MESH,
        )

    def mark_copy(hop):
        source, target = hops[hop]
        return pltpu.make_async_remote_copy(
            src_ref=marks.at[source],
            dst_ref=marks.at[hop],
            send_sem=mark_send.at[hop - 1],
            recv_sem=mark_recv.at[hop - 1],
            device_id={"col": target},
            device_id_type=MESH,
        )

    def send_slot(hop):
        mark_copy(hop).start()
        for part in range(PARTS):
            slot_copy(hop, part).start()

    def receive_slot(hop):
        mark_copy(hop).wait_recv()
        for part in range(PARTS):
            slot_copy(hop, part).wait_recv()

    def forward(part):
        slot_copy(2, part).wait_recv()
        slot_copy(3, part).start()

    def forward_mark():
        mark_copy(2).wait_recv()
        mark_copy(3).start()

    for side in range(2):
        for copy in ghost_copies(side):
            copy.start()

    @pl.when(odd == 0)
    def _():
        send_slot(2)

    send_slot(1)
    lax.fori_loop(height // 2, height, start_a, 0)

    blocks[zero_block] = jnp.zeros((tile, tile), jnp.bfloat16)
    running[pairs] = jnp.zeros((tile, tile), jnp.float32)

    def clear(c, carry):
        for r in range(CB):
            out_ref[r, c] = jnp.zeros((tile, tile), jnp.float32)
        return carry

    lax.fori_loop(0, column_count, clear, 0)

    for side in range(2):
        for copy in ghost_copies(side):
            copy.wait_recv()
        for t in range(capacity):
            j = height + side * capacity + t
            blocks[j] = ghost_in[side, t]
            place = wrap(ghost_in_ids[side, t : t + 1] - start, coarse)
            group = group + jnp.where(listed == j, place_group(place), 0)

    @pl.when(odd == 1)
    def _():
        send_slot(2)

    lane = lax.broadcasted_iota(jnp.int32, listed.shape, 1)
    byte = jnp.where(group == 0, 1, jnp.where(group == 1, 1 << 8, 1 << 16))
    scan = jnp.where(lane < entries, byte, 0)
    step = 1
    while step < entries:
        scan = scan + jnp.where(lane >= step, pltpu.roll(scan, step, 1), 0)
        step *= 2
    total_counts = scan[:, entries - 1 : entries]
    counts = [(total_counts >> (8 * g)) & 255 for g in range(SPAN)]
    sizes = [((c + 1) >> 1) << 1 for c in counts]
    starts = [jnp.zeros_like(sizes[0]), sizes[0], sizes[0] + sizes[1]]
    slot = jnp.zeros_like(listed)
    for g in range(SPAN):
        slot = slot + jnp.where(group == g, starts[g] + ((scan >> (8 * g)) & 255) - 1, 0)
    packed = jnp.zeros_like(listed)
    for m in range(entries):
        packed = packed + jnp.where(
            slot[:, m : m + 1] == lane, (listed[:, m : m + 1] - zero_block) * 32 + m, 0
        )
    chosen = packed & 31
    column = (packed >> 5) + zero_block
    facts = jnp.ones_like(listed)
    for g in range(SPAN):
        facts = jnp.where(2 * lane == starts[g], 0, facts)
    for g in range(SPAN):
        last = jnp.where(counts[g] > 0, ((starts[g] + sizes[g]) >> 1) - 1, pairs)
        facts = jnp.where(lane == 16 + g, last, facts)
    table_v[...] = jnp.where(
        lane < 32,
        chosen,
        jnp.where(lane < 64, pltpu.roll(column, 32, 1), pltpu.roll(facts, 64, 1)),
    )
    table_copy = pltpu.make_async_copy(table_v, table, table_sem)
    table_copy.start()
    table_copy.wait()
    lax.fori_loop(0, height, wait_a, 0)

    def multiply(i, carry):
        total = None
        for pair in range(pairs):
            at = (2 * pair, 2 * pair + 1)
            left = jnp.concatenate([a_buf[i, table[i, n]] for n in at], axis=1)
            right = jnp.concatenate([blocks[table[i, 32 + n]] for n in at], axis=0)
            term = jnp.dot(left, right, preferred_element_type=jnp.float32)
            total = term if pair == 0 else jnp.where(table[i, 64 + pair] > 0, total, 0.0) + term
            running[pair] = total
        rows_of = pl.ds(pl.multiple_of(i * tile, tile), tile)
        for g in range(SPAN):
            grouped[rows_of, g * tile : (g + 1) * tile] = running[table[i, 80 + g]].astype(jnp.bfloat16)

        @pl.when((odd == 0) & (i == height // 2))
        def _():
            forward_mark()
            forward(0)
            forward(1)

        @pl.when((odd == 0) & (i == height * 3 // 4))
        def _():
            forward(2)
            forward(3)

        return carry

    lax.fori_loop(0, height, multiply, 0)

    own_column = first_column(s)

    def part_copy(side, o, wide):
        columns = pl.ds(SPAN - 1, 1) if wide else pl.ds(0, SPAN - 1)
        return pltpu.make_async_remote_copy(
            src_ref=part_out.at[side, o, columns],
            dst_ref=part_in.at[side, o, columns],
            send_sem=part_send.at[side, o, wide],
            recv_sem=part_recv.at[side, o, wide],
            device_id={"row": before if side == 0 else after},
            device_id_type=MESH,
        )

    @pl.when(odd == 1)
    def _():
        forward_mark()
        for part in range(PARTS - 1):
            forward(part)

    receive_slot(1)

    def use_slot(step, carry):
        second = lax.rem(step, 2)
        others = step == 2 * (1 - late) + second

        @pl.when(others & (odd + second == 1))
        def _():
            receive_slot(3)

        @pl.when(others & (odd == 1) & (second == 1))
        def _():
            forward(PARTS - 1)

        index = lax.rem(2 * late + 2 * (step // 2), 4) + odd + second - 2 * odd * second
        total = None
        for part in range(PARTS):
            left = slots[index, part]
            mark = jnp.concatenate(
                [marks[index, part * per_part + n : part * per_part + n + 1] for n in range(per_part)],
                axis=1,
            )
            high = (left.astype(jnp.float32) * mark).astype(jnp.bfloat16)
            left = jnp.concatenate([left - high, high], axis=0)
            depth = per_part * tile
            term = jnp.dot(
                left, grouped[part * depth : (part + 1) * depth], preferred_element_type=jnp.float32
            )
            total = term if total is None else total + term

        @pl.when(step < 2)
        def _():
            for g in range(SPAN):
                columns = slice(g * tile, (g + 1) * tile)
                part_out[0, second, g] = total[:tile, columns].astype(jnp.bfloat16)
                part_out[1, second, g] = total[tile:, columns].astype(jnp.bfloat16)
            for side in range(2):
                part_copy(side, second, 0).start()

            @pl.when(late == 1)
            def _():
                for side in range(2):
                    part_copy(side, second, 1).start()

        @pl.when(step >= 2)
        def _():
            for g in range(SPAN):
                out_ref[second, lax.rem(own_column + g, column_count)] = total[
                    :tile, g * tile : (g + 1) * tile
                ]

        return carry

    lax.fori_loop(0, 4, use_slot, 0)

    columns_in = [first_column(after), first_column(before)]

    def collect(o, carry):
        for side in range(2):

            def add(g):
                at = lax.rem(columns_in[side] + g, column_count)
                out_ref[o, at] = out_ref[o, at] + part_in[side, o, g].astype(jnp.float32)

            part_copy(side, o, 0).wait_recv()
            for g in range(SPAN - 1):
                add(g)

            @pl.when(late == 0)
            def _():
                part_copy(side, o, 1).wait_recv()
                add(SPAN - 1)

        return carry

    lax.fori_loop(0, CB, collect, 0)

    for side in range(2):
        for copy in ghost_copies(side):
            copy.wait_send()
        for o in range(CB):
            part_copy(side, o, 0).wait_send()

    @pl.when(late == 1)
    def _():
        for side in range(2):
            for o in range(CB):
                part_copy(side, o, 1).wait_send()

    for hop in (1, 2, 3):
        mark_copy(hop).wait_send()
        for part in range(PARTS):
            slot_copy(hop, part).wait_send()


def shards(a_tiles, a_cols, p_tiles, p_cols, send_rows):
    rows, cols = lax.axis_size("row"), lax.axis_size("col")
    assert cols == 4
    height, entries, tile, _ = a_tiles.shape
    capacity = send_rows.shape[1]
    column_count = CB * rows // cols
    width = SPAN * tile
    vmem = pl.BlockSpec(memory_space=pltpu.VMEM)
    operands = (a_cols, p_cols.reshape(height), send_rows, p_tiles, a_tiles)
    bf16, f32, i32 = jnp.bfloat16, jnp.float32, jnp.int32
    dma = pltpu.SemaphoreType.DMA
    return pl.pallas_call(
        functools.partial(kernel, rows),
        out_shape=jax.ShapeDtypeStruct((CB, column_count, tile, tile), f32),
        in_specs=[pl.BlockSpec(memory_space=pltpu.HBM)] * 5,
        out_specs=vmem,
        scratch_shapes=[
            pltpu.VMEM(a_cols.shape, i32),
            pltpu.SMEM((height,), i32),
            pltpu.SMEM(send_rows.shape, i32),
            pltpu.VMEM(p_tiles.shape, bf16),
            pltpu.VMEM(a_tiles.shape, bf16),
            pltpu.VMEM((2, capacity, tile, tile), bf16),
            pltpu.VMEM((2, 8, tile), i32),
            pltpu.VMEM((2, capacity, tile, tile), bf16),
            pltpu.VMEM((2, 8, tile), i32),
            pltpu.VMEM((4, PARTS, tile, height // PARTS * tile), bf16),
            pltpu.VMEM((4, height, tile), f32),
            pltpu.VMEM((height + 2 * capacity + 1, tile, tile), bf16),
            pltpu.VMEM(((entries + SPAN) // 2 + 1, tile, tile), f32),
            pltpu.VMEM((height, 128), i32),
            pltpu.VMEM((height, 128), i32),
            pltpu.SMEM((height, 128), i32),
            pltpu.VMEM((height * tile, width), bf16),
            pltpu.VMEM((2, CB, SPAN, tile, tile), bf16),
            pltpu.VMEM((2, CB, SPAN, tile, tile), bf16),
            dma((4,)),
            dma,
            dma((height,)),
            dma((2, 2)),
            dma((2, 2)),
            dma((3, PARTS)),
            dma((3, PARTS)),
            dma((3,)),
            dma((3,)),
            dma((2, CB, 2)),
            dma((2, CB, 2)),
        ],
        compiler_params=pltpu.CompilerParams(
            collective_id=0, has_side_effects=True, vmem_limit_bytes=48 * 1024 * 1024
        ),
        cost_estimate=pl.CostEstimate(
            flops=2 * height * entries * tile * tile * width,
            bytes_accessed=2 * a_tiles.size,
            transcendentals=0,
        ),
    )(*(pltpu.with_memory_space_constraint(x, pltpu.HBM) for x in operands))


def solution(mesh):
    in_specs = (
        P("row", None, None, None),
        P("row", None),
        P("row", "col", None, None),
        P("row", "col"),
        P("row", None),
    )
    out_specs = P("row", "col", None, None)
    return jax.shard_map(shards, mesh=mesh, in_specs=in_specs, out_specs=out_specs, check_vma=False)
```

time: 32.4 us -> 29.5 us (0.910); the launches traced: 32.2 us -> 28.9 us
  Pallas kernels: 31.4 us -> 28.1 us
    pallas_call x1, Pallas kernels: 31.4 us -> 28.1 us  [shards(): pl.pallas_call(functools.partial(kernel, rows), out_shape=jax.ShapeDtypeS...]
where the time goes in v5:
time: 29.5 us; the launch traced here: 28.9 us
  Pallas kernels  28.1 us (95%)
  local copies, waits for them, and re-layouts  0.8 us (3%)
    pallas_call x1, Pallas kernels, shards(): pl.pallas_call(functools.partial(kernel, rows), out_shape=jax.ShapeDtypeS...  28.1 us
    unnamed x1, local copies, waits for them, and re-layouts  0.8 us

profile of v5, /device:TPU:0, one launch (start us, length us, event | category | flops | bytes accessed | tf_op | source)
XLA Modules:
  0.0 28.9 jit_solution(877813983668900266)
XLA Ops:
  0.0 28.1 %shard_map.55 = f32[2,4,128,128]{3,2,1,0:T(8,128)S(1)} custom-call(s32[16,27]{1,0:T(8,128)} %a_cols_ref.1, s32[16]{0:T(128)} %bitcast.1, s32[2,2]{1,0:T(2,128)} %send_rows_ref.1, bf16[16,1,128,128]{3,2,1,0:T(8,128)(2,1)} %p_hbm.1, bf16[16,27,128,128]{3,2,1,0:T(8,128)(2,1)} %a_ref.1), custom_call_target="tpu_custom_call" | custom-call | flops 5435817984 | bytes 14155776 | tf_op jit(solution)/shard_map/pallas_call | solution.py:425
  28.2 0.8 %copy.7 = f32[2,4,128,128]{3,2,1,0:T(8,128)} copy(f32[2,4,128,128]{3,2,1,0:T(8,128)S(1)} %shard_map.55) | data formatting | bytes 1048576

commit v6 on v5

--- a/solution.py
+++ b/solution.py
@@ -37,7 +37,8 @@
     slots,
     marks,
     blocks,
-    running,
+    running_even,
+    running_odd,
     padded,
     table_v,
     table,
@@ -127,19 +128,6 @@
     padded[:, :entries] = a_cols[...]
     listed = padded[...]
 
-    def own_part(part, group):
-        for n in range(per_part):
-            i = part * per_part + n
-            block = p_ref[i, 0]
-            blocks[i] = block
-            slots[0, part, :, n * tile : (n + 1) * tile] = block.T
-            place = wrap(p_cols[i] - left_start, coarse)
-            marks[0, pl.ds(i, 1)] = jnp.full((1, tile), jnp.where(place >= 4, 1.0, 0.0), jnp.float32)
-            group = group + jnp.where(listed == i, place_group(wrap(p_cols[i] - start, coarse)), 0)
-        return group
-
-    group = lax.fori_loop(0, PARTS, own_part, jnp.zeros_like(listed))
-
     pl.semaphore_wait(barrier, 4)
 
     def ghost_copies(side):
@@ -202,15 +190,36 @@
         for copy in ghost_copies(side):
             copy.start()
 
+    def own_part(part, group):
+        for n in range(per_part):
+            i = part * per_part + n
+            block = p_ref[i, 0]
+            blocks[i] = block
+            slots[0, part, :, n * tile : (n + 1) * tile] = block.T
+            place = wrap(p_cols[i] - left_start, coarse)
+            marks[0, pl.ds(i, 1)] = jnp.full((1, tile), jnp.where(place >= 4, 1.0, 0.0), jnp.float32)
+            group = group + jnp.where(listed == i, place_group(wrap(p_cols[i] - start, coarse)), 0)
+
+        @pl.when(odd == 0)
+        def _():
+            slot_copy(2, part).start()
+
+        slot_copy(1, part).start()
+        return group
+
+    group = lax.fori_loop(0, PARTS, own_part, jnp.zeros_like(listed))
+
+    mark_copy(1).start()
+
     @pl.when(odd == 0)
     def _():
-        send_slot(2)
-
-    send_slot(1)
+        mark_copy(2).start()
+
     lax.fori_loop(height // 2, height, start_a, 0)
 
     blocks[zero_block] = jnp.zeros((tile, tile), jnp.bfloat16)
-    running[pairs] = jnp.zeros((tile, tile), jnp.float32)
+    for running in (running_even, running_odd):
+        running[pairs] = jnp.zeros((tile, tile), jnp.float32)
 
     def clear(c, carry):
         for r in range(CB):
@@ -269,7 +278,7 @@
     table_copy.wait()
     lax.fori_loop(0, height, wait_a, 0)
 
-    def multiply(i, carry):
+    def group_row(i, running):
         total = None
         for pair in range(pairs):
             at = (2 * pair, 2 * pair + 1)
@@ -282,6 +291,11 @@
         for g in range(SPAN):
             grouped[rows_of, g * tile : (g + 1) * tile] = running[table[i, 80 + g]].astype(jnp.bfloat16)
 
+    def multiply(both, carry):
+        i = 2 * both
+        group_row(i, running_even)
+        group_row(i + 1, running_odd)
+
         @pl.when((odd == 0) & (i == height // 2))
         def _():
             forward_mark()
@@ -295,7 +309,7 @@
 
         return carry
 
-    lax.fori_loop(0, height, multiply, 0)
+    lax.fori_loop(0, height // 2, multiply, 0)
 
     own_column = first_column(s)
 
@@ -441,6 +455,7 @@
             pltpu.VMEM((4, height, tile), f32),
             pltpu.VMEM((height + 2 * capacity + 1, tile, tile), bf16),
             pltpu.VMEM(((entries + SPAN) // 2 + 1, tile, tile), f32),
+            pltpu.VMEM(((entries + SPAN) // 2 + 1, tile, tile), f32),
             pltpu.VMEM((height, 128), i32),
             pltpu.VMEM((height, 128), i32),
             pltpu.SMEM((height, 128), i32),

time: 29.5 us -> 29 us (0.983)
  the two profiles are of different devices: /device:TPU:0 before, /device:TPU:19 now
where the time goes in v6:
time: 29 us; the launch traced here: 28.9 us
  Pallas kernels  28.1 us (97%)
  local copies, waits for them, and re-layouts  0.8 us (3%)
    pallas_call x1, Pallas kernels, shards(): pl.pallas_call(functools.partial(kernel, rows), out_shape=jax.ShapeDtypeS...  28.1 us
    unnamed x1, local copies, waits for them, and re-layouts  0.8 us

profile of v6, /device:TPU:19, one launch (start us, length us, event | category | flops | bytes accessed | tf_op | source)
XLA Modules:
  0.0 28.9 jit_solution(5695393202114947791)
XLA Ops:
  0.0 28.1 %shard_map.55 = f32[2,4,128,128]{3,2,1,0:T(8,128)S(1)} custom-call(s32[16,27]{1,0:T(8,128)} %a_cols_ref.1, s32[16]{0:T(128)} %bitcast.1, s32[2,2]{1,0:T(2,128)} %send_rows_ref.1, bf16[16,1,128,128]{3,2,1,0:T(8,128)(2,1)} %p_hbm.1, bf16[16,27,128,128]{3,2,1,0:T(8,128)(2,1)} %a_ref.1), custom_call_target="tpu_custom_call" | custom-call | flops 5435817984 | bytes 14155776 | tf_op jit(solution)/shard_map/pallas_call | solution.py:439
  28.1 0.8 %copy.7 = f32[2,4,128,128]{3,2,1,0:T(8,128)} copy(f32[2,4,128,128]{3,2,1,0:T(8,128)S(1)} %shard_map.55) | data formatting | bytes 1048576

commit v7 on v6

--- a/solution.py
+++ b/solution.py
@@ -193,9 +193,9 @@
     def own_part(part, group):
         for n in range(per_part):
             i = part * per_part + n
-            block = p_ref[i, 0]
+            block = p_ref[i, 0].T
             blocks[i] = block
-            slots[0, part, :, n * tile : (n + 1) * tile] = block.T
+            slots[0, part, :, n * tile : (n + 1) * tile] = block
             place = wrap(p_cols[i] - left_start, coarse)
             marks[0, pl.ds(i, 1)] = jnp.full((1, tile), jnp.where(place >= 4, 1.0, 0.0), jnp.float32)
             group = group + jnp.where(listed == i, place_group(wrap(p_cols[i] - start, coarse)), 0)
@@ -233,7 +233,7 @@
             copy.wait_recv()
         for t in range(capacity):
             j = height + side * capacity + t
-            blocks[j] = ghost_in[side, t]
+            blocks[j] = ghost_in[side, t].T
             place = wrap(ghost_in_ids[side, t : t + 1] - start, coarse)
             group = group + jnp.where(listed == j, place_group(place), 0)
 
@@ -282,14 +282,16 @@
         total = None
         for pair in range(pairs):
             at = (2 * pair, 2 * pair + 1)
-            left = jnp.concatenate([a_buf[i, table[i, n]] for n in at], axis=1)
-            right = jnp.concatenate([blocks[table[i, 32 + n]] for n in at], axis=0)
-            term = jnp.dot(left, right, preferred_element_type=jnp.float32)
+            left = jnp.concatenate([blocks[table[i, 32 + n]] for n in at], axis=1)
+            right = jnp.concatenate([a_buf[i, table[i, n]] for n in at], axis=1)
+            term = lax.dot_general(
+                left, right, (((1,), (1,)), ((), ())), preferred_element_type=jnp.float32
+            )
             total = term if pair == 0 else jnp.where(table[i, 64 + pair] > 0, total, 0.0) + term
             running[pair] = total
         rows_of = pl.ds(pl.multiple_of(i * tile, tile), tile)
         for g in range(SPAN):
-            grouped[rows_of, g * tile : (g + 1) * tile] = running[table[i, 80 + g]].astype(jnp.bfloat16)
+            grouped[rows_of, g * tile : (g + 1) * tile] = running[table[i, 80 + g]].T.astype(jnp.bfloat16)
 
     def multiply(both, carry):
         i = 2 * both

time: 29 us -> 29.4 us (1.014)
  the two profiles are of different devices: /device:TPU:19 before, /device:TPU:3 now
where the time goes in v7:
time: 29.4 us; the launch traced here: 29.3 us
  Pallas kernels  28.5 us (97%)
  local copies, waits for them, and re-layouts  0.8 us (3%)
    pallas_call x1, Pallas kernels, shards(): pl.pallas_call(functools.partial(kernel, rows), out_shape=jax.ShapeDtypeS...  28.5 us
    unnamed x1, local copies, waits for them, and re-layouts  0.8 us

profile of v7, /device:TPU:3, one launch (start us, length us, event | category | flops | bytes accessed | tf_op | source)
XLA Modules:
  0.0 29.3 jit_solution(846152470324709572)
XLA Ops:
  0.0 28.5 %shard_map.55 = f32[2,4,128,128]{3,2,1,0:T(8,128)S(1)} custom-call(s32[16,27]{1,0:T(8,128)} %a_cols_ref.1, s32[16]{0:T(128)} %bitcast.1, s32[2,2]{1,0:T(2,128)} %send_rows_ref.1, bf16[16,1,128,128]{3,2,1,0:T(8,128)(2,1)} %p_hbm.1, bf16[16,27,128,128]{3,2,1,0:T(8,128)(2,1)} %a_ref.1), custom_call_target="tpu_custom_call" | custom-call | flops 5435817984 | bytes 14155776 | tf_op jit(solution)/shard_map/pallas_call | solution.py:441
  28.5 0.8 %copy.7 = f32[2,4,128,128]{3,2,1,0:T(8,128)} copy(f32[2,4,128,128]{3,2,1,0:T(8,128)S(1)} %shard_map.55) | data formatting | bytes 1048576

commit v8 on v6

--- a/solution.py
+++ b/solution.py
@@ -29,7 +29,8 @@
     p_cols,
     send_rows,
     p_ref,
-    a_buf,
+    a_low,
+    a_high,
     ghost_out,
     ghost_out_ids,
     ghost_in,
@@ -57,7 +58,7 @@
     part_send,
     part_recv,
 ):
-    height, entries, tile = a_buf.shape[0], a_buf.shape[1], a_buf.shape[2]
+    height, entries, tile = 2 * a_low.shape[0], a_low.shape[1], a_low.shape[2]
     capacity = ghost_out.shape[1]
     coarse = CB * rows
     column_count = out_ref.shape[1]
@@ -90,18 +91,26 @@
     for copy in small:
         copy.start()
 
-    def a_copy(i):
-        return pltpu.make_async_copy(a_ref.at[i], a_buf.at[i], a_sem.at[i])
-
-    def start_a(i, carry):
-        a_copy(i).start()
-        return carry
-
-    def wait_a(i, carry):
-        a_copy(i).wait()
-        return carry
-
-    lax.fori_loop(0, height // 2, start_a, 0)
+    half = height // 2
+
+    def a_copy(target, first, i):
+        return pltpu.make_async_copy(a_ref.at[first + i], target.at[i], a_sem.at[first + i])
+
+    def start_a(target, first):
+        def one(i, carry):
+            a_copy(target, first, i).start()
+            return carry
+
+        lax.fori_loop(0, half, one, 0)
+
+    def wait_a(target, first):
+        def one(i, carry):
+            a_copy(target, first, i).wait()
+            return carry
+
+        lax.fori_loop(0, half, one, 0)
+
+    start_a(a_low, 0)
 
     def first_id(slab):
         return lax.rem(CB * slab + coarse - 4, coarse)
@@ -215,7 +224,7 @@
     def _():
         mark_copy(2).start()
 
-    lax.fori_loop(height // 2, height, start_a, 0)
+    start_a(a_high, half)
 
     blocks[zero_block] = jnp.zeros((tile, tile), jnp.bfloat16)
     for running in (running_even, running_odd):
@@ -276,13 +285,14 @@
     table_copy = pltpu.make_async_copy(table_v, table, table_sem)
     table_copy.start()
     table_copy.wait()
-    lax.fori_loop(0, height, wait_a, 0)
-
-    def group_row(i, running):
+    wait_a(a_low, 0)
+
+    def group_row(source, first, n_row, running):
+        i = first + n_row
         total = None
         for pair in range(pairs):
             at = (2 * pair, 2 * pair + 1)
-            left = jnp.concatenate([a_buf[i, table[i, n]] for n in at], axis=1)
+            left = jnp.concatenate([source[n_row, table[i, n]] for n in at], axis=1)
             right = jnp.concatenate([blocks[table[i, 32 + n]] for n in at], axis=0)
             term = jnp.dot(left, right, preferred_element_type=jnp.float32)
             total = term if pair == 0 else jnp.where(table[i, 64 + pair] > 0, total, 0.0) + term
@@ -291,25 +301,30 @@
         for g in range(SPAN):
             grouped[rows_of, g * tile : (g + 1) * tile] = running[table[i, 80 + g]].astype(jnp.bfloat16)
 
-    def multiply(both, carry):
-        i = 2 * both
-        group_row(i, running_even)
-        group_row(i + 1, running_odd)
-
-        @pl.when((odd == 0) & (i == height // 2))
-        def _():
-            forward_mark()
-            forward(0)
-            forward(1)
-
-        @pl.when((odd == 0) & (i == height * 3 // 4))
-        def _():
-            forward(2)
-            forward(3)
-
-        return carry
-
-    lax.fori_loop(0, height // 2, multiply, 0)
+    def multiply(source, first):
+        def two(both, carry):
+            group_row(source, first, 2 * both, running_even)
+            group_row(source, first, 2 * both + 1, running_odd)
+
+            @pl.when((odd == 0) & (first + 2 * both == height * 3 // 4))
+            def _():
+                forward(2)
+                forward(3)
+
+            return carry
+
+        lax.fori_loop(0, half // 2, two, 0)
+
+    multiply(a_low, 0)
+
+    @pl.when(odd == 0)
+    def _():
+        forward_mark()
+        forward(0)
+        forward(1)
+
+    wait_a(a_high, half)
+    multiply(a_high, half)
 
     own_column = first_column(s)
 
@@ -446,7 +461,8 @@
             pltpu.SMEM((height,), i32),
             pltpu.SMEM(send_rows.shape, i32),
             pltpu.VMEM(p_tiles.shape, bf16),
-            pltpu.VMEM(a_tiles.shape, bf16),
+            pltpu.VMEM((height // 2,) + a_tiles.shape[1:], bf16),
+            pltpu.VMEM((height // 2,) + a_tiles.shape[1:], bf16),
             pltpu.VMEM((2, capacity, tile, tile), bf16),
             pltpu.VMEM((2, 8, tile), i32),
             pltpu.VMEM((2, capacity, tile, tile), bf16),

time: 29 us -> 29.7 us (1.024)
  Pallas kernels: 28.1 us -> 28.8 us
    pallas_call x1, Pallas kernels: 28.1 us -> 28.8 us  [shards(): pl.pallas_call(functools.partial(kernel, rows), out_shape=jax.ShapeDtypeS...]
where the time goes in v8:
time: 29.7 us; the launch traced here: 29.6 us
  Pallas kernels  28.8 us (97%)
  local copies, waits for them, and re-layouts  0.8 us (3%)
    pallas_call x1, Pallas kernels, shards(): pl.pallas_call(functools.partial(kernel, rows), out_shape=jax.ShapeDtypeS...  28.8 us
    unnamed x1, local copies, waits for them, and re-layouts  0.8 us

profile of v8, /device:TPU:19, one launch (start us, length us, event | category | flops | bytes accessed | tf_op | source)
XLA Modules:
  0.0 29.6 jit_solution(12211386943123360520)
XLA Ops:
  0.0 28.8 %shard_map.55 = f32[2,4,128,128]{3,2,1,0:T(8,128)S(1)} custom-call(s32[16,27]{1,0:T(8,128)} %a_cols_ref.1, s32[16]{0:T(128)} %bitcast.1, s32[2,2]{1,0:T(2,128)} %send_rows_ref.1, bf16[16,1,128,128]{3,2,1,0:T(8,128)(2,1)} %p_hbm.1, bf16[16,27,128,128]{3,2,1,0:T(8,128)(2,1)} %a_ref.1), custom_call_target="tpu_custom_call" | custom-call | flops 5435817984 | bytes 14155776 | tf_op jit(solution)/shard_map/pallas_call | solution.py:454
  28.8 0.8 %copy.7 = f32[2,4,128,128]{3,2,1,0:T(8,128)} copy(f32[2,4,128,128]{3,2,1,0:T(8,128)S(1)} %shard_map.55) | data formatting | bytes 1048576

commit v9 on v6

--- a/solution.py
+++ b/solution.py
@@ -168,11 +168,6 @@
             device_id_type=MESH,
         )
 
-    def send_slot(hop):
-        mark_copy(hop).start()
-        for part in range(PARTS):
-            slot_copy(hop, part).start()
-
     def receive_slot(hop):
         mark_copy(hop).wait_recv()
         for part in range(PARTS):
@@ -200,21 +195,14 @@
             marks[0, pl.ds(i, 1)] = jnp.full((1, tile), jnp.where(place >= 4, 1.0, 0.0), jnp.float32)
             group = group + jnp.where(listed == i, place_group(wrap(p_cols[i] - start, coarse)), 0)
 
-        @pl.when(odd == 0)
-        def _():
-            slot_copy(2, part).start()
-
-        slot_copy(1, part).start()
+        for hop in (2, 1):
+            slot_copy(hop, part).start()
         return group
 
     group = lax.fori_loop(0, PARTS, own_part, jnp.zeros_like(listed))
 
-    mark_copy(1).start()
-
-    @pl.when(odd == 0)
-    def _():
-        mark_copy(2).start()
-
+    for hop in (2, 1):
+        mark_copy(hop).start()
     lax.fori_loop(height // 2, height, start_a, 0)
 
     blocks[zero_block] = jnp.zeros((tile, tile), jnp.bfloat16)
@@ -236,10 +224,6 @@
             blocks[j] = ghost_in[side, t]
             place = wrap(ghost_in_ids[side, t : t + 1] - start, coarse)
             group = group + jnp.where(listed == j, place_group(place), 0)
-
-    @pl.when(odd == 1)
-    def _():
-        send_slot(2)
 
     lane = lax.broadcasted_iota(jnp.int32, listed.shape, 1)
     byte = jnp.where(group == 0, 1, jnp.where(group == 1, 1 << 8, 1 << 16))
@@ -296,16 +280,15 @@
         group_row(i, running_even)
         group_row(i + 1, running_odd)
 
-        @pl.when((odd == 0) & (i == height // 2))
+        @pl.when(i == height // 2)
         def _():
             forward_mark()
             forward(0)
             forward(1)
 
-        @pl.when((odd == 0) & (i == height * 3 // 4))
+        @pl.when(i == height * 3 // 4)
         def _():
             forward(2)
-            forward(3)
 
         return carry
 
@@ -324,27 +307,18 @@
             device_id_type=MESH,
         )
 
-    @pl.when(odd == 1)
-    def _():
-        forward_mark()
-        for part in range(PARTS - 1):
-            forward(part)
-
+    forward(PARTS - 1)
     receive_slot(1)
 
     def use_slot(step, carry):
-        second = lax.rem(step, 2)
-        others = step == 2 * (1 - late) + second
-
-        @pl.when(others & (odd + second == 1))
+        from_mate = lax.rem(step, 2)
+        second = odd + from_mate - 2 * odd * from_mate
+
+        @pl.when(step == 2 * (1 - late) + 1)
         def _():
             receive_slot(3)
 
-        @pl.when(others & (odd == 1) & (second == 1))
-        def _():
-            forward(PARTS - 1)
-
-        index = lax.rem(2 * late + 2 * (step // 2), 4) + odd + second - 2 * odd * second
+        index = lax.rem(2 * late + 2 * (step // 2), 4) + from_mate
         total = None
         for part in range(PARTS):
             left = slots[index, part]

time: 29 us -> 30.5 us (1.052)
  the two profiles are of different devices: /device:TPU:19 before, /device:TPU:0 now
where the time goes in v9:
time: 30.5 us; the launch traced here: 30.3 us
  Pallas kernels  29.5 us (97%)
  local copies, waits for them, and re-layouts  0.8 us (3%)
    pallas_call x1, Pallas kernels, shards(): pl.pallas_call(functools.partial(kernel, rows), out_shape=jax.ShapeDtypeS...  29.5 us
    unnamed x1, local copies, waits for them, and re-layouts  0.8 us

profile of v9, /device:TPU:0, one launch (start us, length us, event | category | flops | bytes accessed | tf_op | source)
XLA Modules:
  0.0 30.3 jit_solution(1233795381361619091)
XLA Ops:
  0.0 29.5 %shard_map.55 = f32[2,4,128,128]{3,2,1,0:T(8,128)S(1)} custom-call(s32[16,27]{1,0:T(8,128)} %a_cols_ref.1, s32[16]{0:T(128)} %bitcast.1, s32[2,2]{1,0:T(2,128)} %send_rows_ref.1, bf16[16,1,128,128]{3,2,1,0:T(8,128)(2,1)} %p_hbm.1, bf16[16,27,128,128]{3,2,1,0:T(8,128)(2,1)} %a_ref.1), custom_call_target="tpu_custom_call" | custom-call | flops 5435817984 | bytes 14155776 | tf_op jit(solution)/shard_map/pallas_call | solution.py:413
  29.5 0.8 %copy.7 = f32[2,4,128,128]{3,2,1,0:T(8,128)} copy(f32[2,4,128,128]{3,2,1,0:T(8,128)S(1)} %shard_map.55) | data formatting | bytes 1048576

commit v10 on v6

--- a/solution.py
+++ b/solution.py
@@ -313,13 +313,12 @@
 
     own_column = first_column(s)
 
-    def part_copy(side, o, wide):
-        columns = pl.ds(SPAN - 1, 1) if wide else pl.ds(0, SPAN - 1)
+    def part_copy(side, o, g):
         return pltpu.make_async_remote_copy(
-            src_ref=part_out.at[side, o, columns],
-            dst_ref=part_in.at[side, o, columns],
-            send_sem=part_send.at[side, o, wide],
-            recv_sem=part_recv.at[side, o, wide],
+            src_ref=part_out.at[side, o, g],
+            dst_ref=part_in.at[side, o, g],
+            send_sem=part_send.at[side, o, g],
+            recv_sem=part_recv.at[side, o, g],
             device_id={"row": before if side == 0 else after},
             device_id_type=MESH,
         )
@@ -345,42 +344,38 @@
             forward(PARTS - 1)
 
         index = lax.rem(2 * late + 2 * (step // 2), 4) + odd + second - 2 * odd * second
-        total = None
-        for part in range(PARTS):
-            left = slots[index, part]
-            mark = jnp.concatenate(
-                [marks[index, part * per_part + n : part * per_part + n + 1] for n in range(per_part)],
-                axis=1,
-            )
-            high = (left.astype(jnp.float32) * mark).astype(jnp.bfloat16)
-            left = jnp.concatenate([left - high, high], axis=0)
-            depth = per_part * tile
-            term = jnp.dot(
-                left, grouped[part * depth : (part + 1) * depth], preferred_element_type=jnp.float32
-            )
-            total = term if total is None else total + term
-
-        @pl.when(step < 2)
-        def _():
-            for g in range(SPAN):
-                columns = slice(g * tile, (g + 1) * tile)
-                part_out[0, second, g] = total[:tile, columns].astype(jnp.bfloat16)
-                part_out[1, second, g] = total[tile:, columns].astype(jnp.bfloat16)
-            for side in range(2):
-                part_copy(side, second, 0).start()
-
-            @pl.when(late == 1)
+        def one_column(g, inner):
+            lanes = pl.ds(pl.multiple_of(g * tile, tile), tile)
+            total = None
+            for part in range(PARTS):
+                left = slots[index, part]
+                mark = jnp.concatenate(
+                    [marks[index, part * per_part + n : part * per_part + n + 1] for n in range(per_part)],
+                    axis=1,
+                )
+                high = left * mark.astype(jnp.bfloat16)
+                left = jnp.concatenate([left - high, high], axis=0)
+                depth = per_part * tile
+                term = jnp.dot(
+                    left,
+                    grouped[part * depth : (part + 1) * depth, lanes],
+                    preferred_element_type=jnp.float32,
+                )
+                total = term if total is None else total + term
+
+            @pl.when(step < 2)
             def _():
                 for side in range(2):
-                    part_copy(side, second, 1).start()
-
-        @pl.when(step >= 2)
-        def _():
-            for g in range(SPAN):
-                out_ref[second, lax.rem(own_column + g, column_count)] = total[
-                    :tile, g * tile : (g + 1) * tile
-                ]
-
+                    part_out[side, second, g] = total[side * tile : (side + 1) * tile].astype(jnp.bfloat16)
+                    part_copy(side, second, g).start()
+
+            @pl.when(step >= 2)
+            def _():
+                out_ref[second, lax.rem(own_column + g, column_count)] = total[:tile]
+
+            return inner
+
+        lax.fori_loop(0, SPAN - 1 + late, one_column, 0)
         return carry
 
     lax.fori_loop(0, 4, use_slot, 0)
@@ -388,21 +383,14 @@
     columns_in = [first_column(after), first_column(before)]
 
     def collect(o, carry):
-        for side in range(2):
-
-            def add(g):
+        def add(g, inner):
+            for side in range(2):
+                part_copy(side, o, g).wait_recv()
                 at = lax.rem(columns_in[side] + g, column_count)
                 out_ref[o, at] = out_ref[o, at] + part_in[side, o, g].astype(jnp.float32)
-
-            part_copy(side, o, 0).wait_recv()
-            for g in range(SPAN - 1):
-                add(g)
-
-            @pl.when(late == 0)
-            def _():
-                part_copy(side, o, 1).wait_recv()
-                add(SPAN - 1)
-
+            return inner
+
+        lax.fori_loop(0, SPAN - late, add, 0)
         return carry
 
     lax.fori_loop(0, CB, collect, 0)
@@ -410,15 +398,14 @@
     for side in range(2):
         for copy in ghost_copies(side):
             copy.wait_send()
-        for o in range(CB):
-            part_copy(side, o, 0).wait_send()
-
-    @pl.when(late == 1)
-    def _():
+
+    def sent(g, carry):
         for side in range(2):
             for o in range(CB):
-                part_copy(side, o, 1).wait_send()
-
+                part_copy(side, o, g).wait_send()
+        return carry
+
+    lax.fori_loop(0, SPAN - 1 + late, sent, 0)
     for hop in (1, 2, 3):
         mark_copy(hop).wait_send()
         for part in range(PARTS):
@@ -471,8 +458,8 @@
             dma((3, PARTS)),
             dma((3,)),
             dma((3,)),
-            dma((2, CB, 2)),
-            dma((2, CB, 2)),
+            dma((2, CB, SPAN)),
+            dma((2, CB, SPAN)),
         ],
         compiler_params=pltpu.CompilerParams(
             collective_id=0, has_side_effects=True, vmem_limit_bytes=48 * 1024 * 1024

time: 29 us -> 29.4 us (1.014)
  the two profiles are of different devices: /device:TPU:19 before, /device:TPU:0 now
where the time goes in v10:
time: 29.4 us; the launch traced here: 29.3 us
  Pallas kernels  28.5 us (97%)
  local copies, waits for them, and re-layouts  0.8 us (3%)
    pallas_call x1, Pallas kernels, shards(): pl.pallas_call(functools.partial(kernel, rows), out_shape=jax.ShapeDtypeS...  28.5 us
    unnamed x1, local copies, waits for them, and re-layouts  0.8 us

profile of v10, /device:TPU:0, one launch (start us, length us, event | category | flops | bytes accessed | tf_op | source)
XLA Modules:
  0.0 29.3 jit_solution(18109874419148471385)
XLA Ops:
  0.0 28.5 %shard_map.55 = f32[2,4,128,128]{3,2,1,0:T(8,128)S(1)} custom-call(s32[16,27]{1,0:T(8,128)} %a_cols_ref.1, s32[16]{0:T(128)} %bitcast.1, s32[2,2]{1,0:T(2,128)} %send_rows_ref.1, bf16[16,1,128,128]{3,2,1,0:T(8,128)(2,1)} %p_hbm.1, bf16[16,27,128,128]{3,2,1,0:T(8,128)(2,1)} %a_ref.1), custom_call_target="tpu_custom_call" | custom-call | flops 5435817984 | bytes 14155776 | tf_op jit(solution)/shard_map/pallas_call | solution.py:426
  28.5 0.8 %copy.7 = f32[2,4,128,128]{3,2,1,0:T(8,128)} copy(f32[2,4,128,128]{3,2,1,0:T(8,128)S(1)} %shard_map.55) | data formatting | bytes 1048576

commit v11 on v6

--- a/solution.py
+++ b/solution.py
@@ -237,10 +237,6 @@
             place = wrap(ghost_in_ids[side, t : t + 1] - start, coarse)
             group = group + jnp.where(listed == j, place_group(place), 0)
 
-    @pl.when(odd == 1)
-    def _():
-        send_slot(2)
-
     lane = lax.broadcasted_iota(jnp.int32, listed.shape, 1)
     byte = jnp.where(group == 0, 1, jnp.where(group == 1, 1 << 8, 1 << 16))
     scan = jnp.where(lane < entries, byte, 0)
@@ -276,6 +272,11 @@
     table_copy = pltpu.make_async_copy(table_v, table, table_sem)
     table_copy.start()
     table_copy.wait()
+
+    @pl.when(odd == 1)
+    def _():
+        send_slot(2)
+
     lax.fori_loop(0, height, wait_a, 0)
 
     def group_row(i, running):

time: 29 us -> 28.7 us (0.990)
  the two profiles are of different devices: /device:TPU:19 before, /device:TPU:2 now
where the time goes in v11:
time: 28.7 us; the launch traced here: 28.6 us
  Pallas kernels  27.7 us (97%)
  local copies, waits for them, and re-layouts  0.8 us (3%)
    pallas_call x1, Pallas kernels, shards(): pl.pallas_call(functools.partial(kernel, rows), out_shape=jax.ShapeDtypeS...  27.7 us
    unnamed x1, local copies, waits for them, and re-layouts  0.8 us

profile of v11, /device:TPU:2, one launch (start us, length us, event | category | flops | bytes accessed | tf_op | source)
XLA Modules:
  0.0 28.6 jit_solution(5730535448926964263)
XLA Ops:
  0.0 27.7 %shard_map.55 = f32[2,4,128,128]{3,2,1,0:T(8,128)S(1)} custom-call(s32[16,27]{1,0:T(8,128)} %a_cols_ref.1, s32[16]{0:T(128)} %bitcast.1, s32[2,2]{1,0:T(2,128)} %send_rows_ref.1, bf16[16,1,128,128]{3,2,1,0:T(8,128)(2,1)} %p_hbm.1, bf16[16,27,128,128]{3,2,1,0:T(8,128)(2,1)} %a_ref.1), custom_call_target="tpu_custom_call" | custom-call | flops 5435817984 | bytes 14155776 | tf_op jit(solution)/shard_map/pallas_call | solution.py:440
  27.8 0.8 %copy.7 = f32[2,4,128,128]{3,2,1,0:T(8,128)} copy(f32[2,4,128,128]{3,2,1,0:T(8,128)S(1)} %shard_map.55) | data formatting | bytes 1048576
